TPU v7x, 32 devices: a whole 2x2x4 slice. The times are simulated.
32 devices in a mesh: row: 4 (over y, core), col: 8 (over z, x).
Axes of the slice: x: 2, y: 2, z: 4, core: 2. Of those that a mesh axis runs over, the one named last changes fastest.
Arguments:
- transition: bfloat16 [32768, 32768], P('row', 'col'), may hold values from 1.5258789e-06 to 0.0024414062, as said below
- emission: bfloat16 [96, 32768], P(None, 'col'), may hold values from 0.0099487305 to 1
- token_ids: int32 [2, 192], replicated, may hold values from 0 to 95
- forward: bfloat16 [2, 192, 32768], P(None, 'col', 'row'), may hold values from 3.0517578e-06 to 0.0008239746, as said below
- backward_last: float32 [192, 32768], P('row', 'col'), may hold values from 0.1 to 10
Outputs:
- backward: float32 [2, 192, 32768], P(None, 'col', 'row')
- counts: float32 [32768, 1024], P('row', 'col')
Inputs may be any that keep to these rules, and one draw needn't show every extreme that they name: Positive transition weights. Positive forward weights.
All inputs are finite; a program needn't handle non-finite values.
Results may differ from a plain program's by a relative error of at most 0.00048.
Values may be sent and summed in bfloat16 or wider, within the bound.
A program may use at most 192 MiB of HBM per device.

v0:
```python
import jax
import jax.numpy as jnp
from jax import lax
from jax.sharding import PartitionSpec as P

H = 32768
N = 192
DW = 128


def spread(value, axis, source):
    kept = jnp.where(lax.axis_index(axis) == source, value, 0).astype(value.dtype)
    return lax.psum(kept, axis)


def on_device(transition, emission, token_ids, forward, backward_last):
    row_count = lax.axis_size("row")
    col_count = lax.axis_size("col")
    col_index = lax.axis_index("col")
    ratio = col_count // row_count
    local_seqs = forward.shape[1]
    block_src = transition.shape[0]
    block_dst = transition.shape[1]
    seq_total = local_seqs * col_count
    forward_all = lax.all_gather(forward, "col", axis=1, tiled=True)
    backward_next = lax.all_gather(backward_last, "row", axis=0, tiled=True)
    columns = lax.broadcasted_iota(jnp.int32, (seq_total, emission.shape[0]), 1)
    window = transition[:, :DW]
    totals = jnp.zeros((block_src, DW), jnp.float32)
    outputs = [None, None]
    for step in (1, 0):
        onehot = (token_ids[step][:, None] == columns).astype(jnp.bfloat16)
        emitted = jnp.dot(onehot, emission, preferred_element_type=jnp.float32)
        weighted_back = (emitted * backward_next).astype(jnp.bfloat16)
        partial_value = lax.dot_general(
            weighted_back, transition, (((1,), (1,)), ((), ())), preferred_element_type=jnp.float32
        )
        alpha_all = forward_all[step].astype(jnp.float32)
        summed = lax.psum(partial_value, "col")
        mine = lax.dynamic_slice_in_dim(summed, col_index * local_seqs, local_seqs, 0)
        alpha_mine = forward[step].astype(jnp.float32)
        local_norm = lax.psum(jnp.sum(alpha_mine * mine, axis=1), "row")
        normal_all = lax.all_gather(local_norm, "col", axis=0, tiled=True)
        normal_mine = lax.dynamic_slice_in_dim(normal_all, col_index * local_seqs, local_seqs, 0)
        outputs[step] = mine / normal_mine[:, None]
        scaled = (alpha_all / normal_all[:, None]).astype(jnp.bfloat16)
        totals = totals + lax.dot_general(
            scaled,
            weighted_back[:, :DW],
            (((0,), (0,)), ((), ())),
            preferred_element_type=jnp.float32,
        )
        if step == 1:
            whole = summed / normal_all[:, None]
            piece = lax.dynamic_slice_in_dim(whole, col_index % ratio * block_dst, block_dst, 1)
            backward_next = spread(piece, "row", col_index // ratio)
    counts = window.astype(jnp.float32) * totals * (H * H / N)
    return (jnp.stack(outputs), counts)


def solution(mesh):
    in_specs = (P("row", "col"), P(None, "col"), P(), P(None, "col", "row"), P("row", "col"))
    out_specs = (P(None, "col", "row"), P("row", "col"))
    return jax.shard_map(
        on_device, mesh=mesh, in_specs=in_specs, out_specs=out_specs, check_vma=False
    )
```

profile of v0, /device:TPU:0, one launch (start us, length us, event | category | flops | bytes accessed | tf_op | source)
XLA Modules:
  0.0 741.6 jit_solution(9007567216397277755)
XLA Ops:
  7.2 0.7 all-gather.3.cloned.1.call-update
  8.0 0.8 fusion.17
  8.7 32.1 %all-gather.3.cloned.1.call-done = f32[192,4096]{1,0:T(8,128)} async-done(((f32[48,4096]{1,0:T(8,128)}), f32[192,4096]{1,0:T(8,128)}) %all-gather.3.cloned.1.call-update) | async-done | bytes 3145744 | tf_op jit(solution)/shard_map/all_gather | solution.py:26
  40.8 2.5 fusion.5
  43.3 31.1 %fusion.18 = f32[192,8192]{1,0:T(8,128)} fusion(bf16[192,4096]{1,0:T(8,128)(2,1)S(1)} %fusion.5, bf16[8192,4096]{1,0:T(8,128)(2,1)} %param.5), kind=kOutput, calls=%fused_computation.31 | convolution fusion | flops 12884901888 | bytes 74973184 | tf_op jit(solution)/shard_map/dot_general | solution.py:35
  74.5 0.0 all-reduce.8.cloned.1.call-start
  74.6 0.6 copy-done.3
  75.1 0.6 dynamic-slice
  76.4 209.8 %all-reduce.6.cloned.1.call-done = f32[192,8192]{1,0:T(8,128)} async-done(((f32[192,8192]{1,0:T(8,128)}), f32[192,8192]{1,0:T(8,128)}) %all-reduce.6.cloned.1.call-update) | async-done | bytes 6291472 | tf_op jit(solution)/shard_map/psum | solution.py:39
  286.2 1.3 fusion.12
  287.5 6.9 psum.36
  294.4 0.2 dynamic-update-slice
  294.7 19.4 %all-reduce = f32[192]{0:T(256)S(1)} all-reduce(f32[192]{0:T(256)S(1)} %dynamic-update-slice), channel_id=1, replica_groups=mesh['row'=4,'col'=8] {'col'}, use_global_device_ids=true, to_apply=%add | all-reduce | flops 192 | bytes 1536
  314.1 4.0 fusion.7
  318.1 0.0 all-gather.5.cloned.1.call-start
  318.1 0.5 all-gather.5.cloned.1.call-update
  318.7 64.3 %all-reduce.8.cloned.1.call-done = f32[192,4096]{1,0:T(8,128)} async-done(((f32[192,4096]{1,0:T(8,128)}), f32[192,4096]{1,0:T(8,128)}) %all-reduce.8.cloned.1.call-update) | async-done | bytes 3145744 | tf_op jit(solution)/shard_map/psum | solution.py:13
  383.0 3.7 fusion.4
  386.7 30.8 %fusion.19 = f32[192,8192]{1,0:T(8,128)} fusion(bf16[192,4096]{1,0:T(8,128)(2,1)} %fusion.4, bf16[8192,4096]{1,0:T(8,128)(2,1)} %param.5), kind=kOutput, calls=%fused_computation.32 | convolution fusion | flops 12884901888 | bytes 74973184 | tf_op jit(solution)/shard_map/dot_general | solution.py:35
  417.5 0.1 dynamic_slice.19
  417.6 66.8 %all-gather.5.cloned.1.call-done = bf16[2,192,8192]{2,1,0:T(8,128)(2,1)} async-done(((bf16[2,24,8192]{2,1,0:T(8,128)(2,1)}), bf16[2,192,8192]{2,1,0:T(8,128)(2,1)}) %all-gather.5.cloned.1.call-update) | async-done | bytes 6291472 | tf_op jit(solution)/shard_map/all_gather | solution.py:25
  484.4 5.4 fusion.9
  489.9 1.3 divide_bitcast_fusion
  491.1 207.2 %all-reduce.10.cloned.1.call-done = f32[192,8192]{1,0:T(8,128)} async-done(((f32[192,8192]{1,0:T(8,128)}), f32[192,8192]{1,0:T(8,128)}) %all-reduce.10.cloned.1.call-update) | async-done | bytes 6291472 | tf_op jit(solution)/shard_map/psum | solution.py:39
  698.3 1.3 fusion.11
  699.6 6.9 psum.39
  706.5 0.2 dynamic-update-slice.1
  706.7 19.4 %all-reduce.1 = f32[192]{0:T(256)S(1)} all-reduce(f32[192]{0:T(256)S(1)} %dynamic-update-slice.1), channel_id=1, replica_groups=mesh['row'=4,'col'=8] {'col'}, use_global_device_ids=true, to_apply=%add.1 | all-reduce | flops 192 | bytes 1536
  726.2 0.1 dynamic_slice.18
  726.2 1.4 divide_bitcast_fusion.1
  727.6 1.2 pad_maximum_fusion
  728.9 6.2 fusion.1
  (17 shorter events, 0.2 us)
Async XLA Ops:
  7.2 33.7 %copy-start = (bf16[96,4096]{1,0:T(8,128)(2,1)S(1)}, bf16[96,4096]{1,0:T(8,128)(2,1)}, u32[]{:S(2)}) copy-start(bf16[96,4096]{1,0:T(8,128)(2,1)} %param.6) | copy-start | bytes 2359300
  7.2 33.7 %all-gather.3.cloned.1.call-start = ((), (), s32[]{:S(2)}) async-start(), calls=%async_computation | async-start | bytes 3932160 | tf_op jit(solution)/shard_map/all_gather | solution.py:26
  7.9 278.3 %all-reduce.6.cloned.1.call-start = ((), (), s32[]{:S(2)}) async-start(), calls=%async_computation.1 | async-start | bytes 12582912 | tf_op jit(solution)/shard_map/psum | solution.py:39
  74.5 0.7 copy-start.3
  74.5 211.8 %copy-start.1 = (bf16[2,24,8192]{2,1,0:T(8,128)(2,1)S(1)}, bf16[2,24,8192]{2,1,0:T(8,128)(2,1)}, u32[]{:S(2)}) copy-start(bf16[2,24,8192]{2,1,0:T(8,128)(2,1)} %param.8) | copy-start | bytes 2359300
  74.5 308.5 %all-reduce.8.cloned.1.call-start = ((), (), s32[]{:S(2)}) async-start(), calls=%async_computation.2 | async-start | bytes 6291456 | tf_op jit(solution)/shard_map/psum | solution.py:13
  318.1 166.4 %all-gather.5.cloned.1.call-start = ((), (), s32[]{:S(2)}) async-start(), calls=%async_computation.4 | async-start | bytes 7077888 | tf_op jit(solution)/shard_map/all_gather | solution.py:25
  318.7 379.7 %all-reduce.10.cloned.1.call-start = ((), (), s32[]{:S(2)}) async-start(), calls=%async_computation.3 | async-start | bytes 12582912 | tf_op jit(solution)/shard_map/psum | solution.py:39
  417.6 280.7 %copy-start.2 = (bf16[2,24,8192]{2,1,0:T(8,128)(2,1)S(1)}, bf16[2,24,8192]{2,1,0:T(8,128)(2,1)}, u32[]{:S(2)}) copy-start(bf16[2,24,8192]{2,1,0:T(8,128)(2,1)} %param.8) | copy-start | bytes 2359300
  726.1 2.7 copy-start.4
Sparse Core Ops, SparseCore 0:
  9.6 31.2 all-gather.2
  74.6 211.5 all-reduce.5
  318.2 64.7 all-reduce.7
  385.3 99.1 all-gather.4
  488.5 209.7 all-reduce.9
where the time goes:
time: 742 us
  waiting for transfers between devices  582 us (78%)
  matrix products  79.7 us (11%)
  blocking collectives  52.5 us (7%)
  between operations  14.5 us (2%)
  other arithmetic  10.5 us (1%)
    psum x2, waiting for transfers between devices, on_device(): summed = lax.psum(partial_value, 'col')  417 us
    all_gather x1, waiting for transfers between devices, on_device(): forward_all = lax.all_gather(forward, 'col', axis=1, tiled=True)  66.8 us
    psum x1, waiting for transfers between devices, spread(): return lax.psum(kept, axis)  64.3 us
    dot_general x2, matrix products, on_device(): lax.dot_general(weighted_back, transition, (((1,), (1,)), ((), ())), pref...  61.9 us
    unnamed x2, blocking collectives  38.8 us
    all_gather x1, waiting for transfers between devices, on_device(): backward_next = lax.all_gather(backward_last, 'row', axis=0, tiled=True)  32.1 us
  transfers between devices with their start and end apart: 5, of which 5 were waited for; matrix products, arithmetic and copies ran while one was open for 6% of the time, Pallas kernels for 0%

commit v1 on v0

v1 whole, which is shorter than its diff:
```python
import jax
import jax.numpy as jnp
from jax import lax
from jax.sharding import PartitionSpec as P

H = 32768
N = 192
DW = 128
CHUNKS = 2


def reduce_scatter(partial, scale, col_count, col_index, local_seqs):
    half = col_count // 2
    width = partial.shape[1]
    scaled = (partial * scale).reshape(half, 2, local_seqs, width)
    side = col_index % 2
    away = lax.dynamic_index_in_dim(scaled, 1 - side, 1, keepdims=False).astype(jnp.float16)
    got = lax.ppermute(away, "col", [(c, c ^ 1) for c in range(col_count)])
    pair = lax.dynamic_index_in_dim(scaled, side, 1, keepdims=False) + got.astype(jnp.float32)
    here = col_index // 2
    total = lax.dynamic_index_in_dim(pair, here, 0, keepdims=False)
    packed = pair.astype(jnp.float16)
    for k in range(1, half):
        piece = lax.dynamic_index_in_dim(packed, (here + k) % half, 0, keepdims=False)
        got = lax.ppermute(piece, "col", [(c, (c + 2 * k) % col_count) for c in range(col_count)])
        total = total + got.astype(jnp.float32)
    return total


def on_device(transition, emission, token_ids, forward, backward_last):
    row_count = lax.axis_size("row")
    col_count = lax.axis_size("col")
    row_index = lax.axis_index("row")
    col_index = lax.axis_index("col")
    ratio = col_count // row_count
    local_seqs = forward.shape[1]
    row_seqs = backward_last.shape[0]
    block_src = transition.shape[0]
    block_dst = transition.shape[1]
    seq_total = local_seqs * col_count
    forward_all = [None, lax.all_gather(forward[1], "col", axis=0, tiled=True)]
    columns = lax.broadcasted_iota(jnp.int32, (row_seqs, emission.shape[0]), 1)
    window = transition[:, :DW]
    totals = jnp.zeros((block_src, DW), jnp.float32)
    outputs = [None, None]
    beta = backward_last
    scale = jnp.full((seq_total, 1), 64.0, jnp.float32)
    chunk = block_src // CHUNKS
    for step in (1, 0):
        tokens = lax.dynamic_slice_in_dim(token_ids[step], row_index * row_seqs, row_seqs, 0)
        onehot = (tokens[:, None] == columns).astype(jnp.bfloat16)
        emitted = jnp.dot(onehot, emission, preferred_element_type=jnp.float32)
        local_back = (emitted * beta).astype(jnp.bfloat16)
        weighted_back = lax.all_gather(local_back, "row", axis=0, tiled=True)
        pieces = []
        norm = jnp.zeros((seq_total,), jnp.float32)
        mass = jnp.zeros((seq_total,), jnp.float32)
        if step == 0:
            forward_all[0] = lax.all_gather(forward[0], "col", axis=0, tiled=True)
        for k in range(CHUNKS):
            rows = slice(k * chunk, (k + 1) * chunk)
            partial = lax.dot_general(
                weighted_back, transition[rows], (((1,), (1,)), ((), ())), preferred_element_type=jnp.float32
            )
            norm = norm + jnp.sum(forward_all[step][:, rows].astype(jnp.float32) * partial, axis=1)
            mass = mass + jnp.sum(partial, axis=1)
            pieces.append(reduce_scatter(partial, scale, col_count, col_index, local_seqs))
        if step == 1:
            both = lax.psum(jnp.stack([norm, mass]), ("row", "col"))
            normal_all = both[0]
        else:
            normal_all = lax.psum(norm, ("row", "col"))
        normal_mine = lax.dynamic_slice_in_dim(normal_all, col_index * local_seqs, local_seqs, 0)
        scale_mine = lax.dynamic_slice_in_dim(scale, col_index * local_seqs, local_seqs, 0)
        mine = jnp.concatenate(pieces, axis=1) / (scale_mine * normal_mine[:, None])
        outputs[step] = mine
        if step == 1:
            halves = mine.reshape(local_seqs, ratio, block_dst)
            arrived = []
            for p in range(ratio):
                part = lax.dynamic_index_in_dim(halves, (col_index + p) % ratio, 1, keepdims=False)
                moves = []
                for r in range(row_count):
                    for c in range(col_count):
                        h = (c + p) % ratio
                        moves.append((r * col_count + c, (c // ratio) * col_count + r * ratio + h))
                arrived.append(lax.ppermute(part, ("row", "col"), moves))
            turned = jnp.stack([arrived[-i % ratio] for i in range(ratio)] * 2)
            start = (ratio - col_index % ratio) % ratio
            beta = lax.dynamic_slice_in_dim(turned, start, ratio, 0).reshape(row_seqs, block_dst)
            scale = (16777216.0 * both[0] / both[1])[:, None]
        scaled = (forward_all[step].astype(jnp.float32) / normal_all[:, None]).astype(jnp.bfloat16)
        totals = totals + lax.dot_general(
            scaled, weighted_back[:, :DW], (((0,), (0,)), ((), ())), preferred_element_type=jnp.float32
        )
    counts = window.astype(jnp.float32) * totals * (H * H / N)
    return (jnp.stack(outputs), counts)


def solution(mesh):
    in_specs = (P("row", "col"), P(None, "col"), P(), P(None, "col", "row"), P("row", "col"))
    out_specs = (P(None, "col", "row"), P("row", "col"))
    return jax.shard_map(
        on_device, mesh=mesh, in_specs=in_specs, out_specs=out_specs, check_vma=False
    )
```

time: 742 us -> 470 us (0.63)
  waiting for transfers between devices: 582 us -> 208 us
  blocking collectives: 52.5 us -> 105 us
  starting transfers between devices: 0.2 us -> 29 us
  matrix products: 79.7 us -> 98.1 us
    psum x3 -> x0, waiting for transfers between devices: 481 us -> none  [the longest x2 417 us: on_device(): summed = lax.psum(partial_value, 'col')]
    psum x2, blocking collectives: 13.7 us -> 105 us  [the longest x1 65.4 us: on_device(): both = lax.psum(jnp.stack([norm, mass]), ('row', 'col'))]
    ppermute x0 -> x18, waiting for transfers between devices: none -> 71.9 us  [the longest x12 35.8 us: reduce_scatter(): lax.ppermute(piece, 'col', [(c, (c + 2 * k) % col_count) for c in range(c...]
    unnamed x2 -> x0, blocking collectives: 38.8 us -> none
    all_gather x2 -> x4, waiting for transfers between devices: 98.9 us -> 136 us  [the longest x2 52.4 us: on_device(): weighted_back = lax.all_gather(local_back, 'row', axis=0, tiled=True)]
    ppermute x0 -> x18, starting transfers between devices: none -> 28.7 us  [the longest x12 22.1 us: reduce_scatter(): lax.ppermute(piece, 'col', [(c, (c + 2 * k) % col_count) for c in range(c...]
    dot_general x2 -> x4, matrix products: 61.9 us -> 82.8 us  [on_device(): lax.dot_general(weighted_back, transition[rows], (((1,), (1,)), ((), ()))...]
    convert_element_type x0 -> x8, other arithmetic: none -> 9.57 us  [the longest x4 7.03 us: reduce_scatter(): lax.dynamic_index_in_dim(scaled, 1 - side, 1, keepdims=False)]
  transfers between devices with their start and end apart: 5 -> 22, of which waited for: 5 -> 13; matrix products, arithmetic and copies ran while one was open for 6% -> 13% of each run, Pallas kernels for 0% -> 0%
where the time goes in v1:
time: 470 us; the launch traced here: 469 us
  waiting for transfers between devices  208 us (44%)
  blocking collectives  105 us (22%)
  matrix products  98.1 us (21%)
  starting transfers between devices  29 us (6%)
  between operations  14.1 us (3%)
  other arithmetic  11.9 us (3%)
    dot_general x4, matrix products, on_device(): lax.dot_general(weighted_back, transition[rows], (((1,), (1,)), ((), ()))...  82.8 us
    psum x1, blocking collectives, on_device(): both = lax.psum(jnp.stack([norm, mass]), ('row', 'col'))  65.4 us
    all_gather x2, waiting for transfers between devices, on_device(): weighted_back = lax.all_gather(local_back, 'row', axis=0, tiled=True)  52.4 us
    all_gather x1, waiting for transfers between devices, on_device(): forward_all = [None, lax.all_gather(forward[1], 'col', axis=0, tiled=True)]  42 us
    all_gather x1, waiting for transfers between devices, on_device(): forward_all[0] = lax.all_gather(forward[0], 'col', axis=0, tiled=True)  41.2 us
    psum x1, blocking collectives, on_device(): normal_all = lax.psum(norm, ('row', 'col'))  39.2 us
    ppermute x12, waiting for transfers between devices, reduce_scatter(): lax.ppermute(piece, 'col', [(c, (c + 2 * k) % col_count) for c in range(c...  35.8 us
    ppermute x4, waiting for transfers between devices, reduce_scatter(): got = lax.ppermute(away, 'col', [(c, c ^ 1) for c in range(col_count)])  22.7 us
  transfers between devices with their start and end apart: 22, of which 13 were waited for; matrix products, arithmetic and copies ran while one was open for 13% of the time, Pallas kernels for 0%

profile of v1, /device:TPU:0, one launch (start us, length us, event | category | flops | bytes accessed | tf_op | source)
XLA Modules:
  0.0 469.5 jit_solution(5049262565942433598)
XLA Ops:
  8.3 2.2 fusion.10
  10.6 2.0 fusion.50
  12.8 20.2 %all-gather.7.cloned.1.call-done = bf16[192,4096]{1,0:T(8,128)(2,1)} async-done(((bf16[48,4096]{1,0:T(8,128)(2,1)}), bf16[192,4096]{1,0:T(8,128)(2,1)}) %all-gather.7.cloned.1.call-update) | async-done | bytes 1572880 | tf_op jit(solution)/shard_map/all_gather | solution.py:54
  33.1 21.2 %fusion.6 = f32[192,4096]{1,0:T(8,128)} fusion(bf16[192,4096]{1,0:T(8,128)(2,1)} %all-gather.7.cloned.1.call-done, bf16[8192,4096]{1,0:T(8,128)(2,1)} %param.5), kind=kOutput, calls=%fused_computation.6 | convolution fusion | flops 6442450944 | bytes 38273024 | tf_op jit(solution)/shard_map/dot_general | solution.py:62
  54.3 42.0 %all-gather.11.cloned.1.call-done = bf16[1,192,8192]{2,1,0:T(8,128)(2,1)} async-done(((bf16[1,24,8192]{2,1,0:T(8,128)(2,1)}), bf16[1,192,8192]{2,1,0:T(8,128)(2,1)}) %all-gather.11.cloned.1.call-update) | async-done | bytes 3145744 | tf_op jit(solution)/shard_map/all_gather | solution.py:41
  96.3 20.1 %multiply_reduce_fusion.2 = (f32[192]{0:T(256)S(1)}, f32[192]{0:T(256)S(1)}, f32[192]{0:T(256)S(1)}, f32[192]{0:T(256)S(1)}, f32[192,4096]{1,0:T(8,128)}, /*index=5*/f32[192,4096]{1,0:T(8,128)}) fusion(bf16[192,8192]{1,0:T(8,128)(2,1)} %bitcast.147, f32[192,4096]{1,0:T(8,128)} %fusion.6, bf16[192,4096]{1,0:T(8,128)(2,1)S(1)} %copy-done.6, ...), kind=kOutput, calls=%fused_computation.18 | convolution fusion | flops 6450315264 | bytes 47713280 | tf_op jit(solution)/shard_map/dot_general | solution.py:62
  116.4 2.4 fusion.14
  120.9 1.5 collective-permute-start
  122.4 65.4 %psum.14 = f32[2,192]{1,0:T(2,128)S(1)} all-reduce(f32[2,192]{1,0:T(2,128)S(1)} %pad_maximum_fusion.1), channel_id=1, replica_groups=mesh['row'=4,'col'=8] {'row','col'}, use_global_device_ids=true, to_apply=%region_4.5 | all-reduce | flops 384 | bytes 3072 | tf_op jit(solution)/shard_map/psum | solution.py:69
  188.0 1.8 fusion.49
  190.8 2.9 collective-permute-start.7
  194.8 3.3 collective-permute-start.3
  198.0 1.5 collective-permute-done.5
  199.6 6.6 %collective-permute-start.2 = (f16[24,4096]{1,0:T(8,128)(2,1)S(1)}, f16[24,4096]{1,0:T(8,128)(2,1)S(1)}, u32[]{:S(2)}, u32[]{:S(2)}) collective-permute-start(f16[24,4096]{1,0:T(8,128)(2,1)S(1)} %get-tuple-element.36), channel_id=1, source_target_pairs={{0,4},{1,5},{2,6},{3,7},{4,0},{5,1},{6,2},{7,3},{8,12},{9,13},{10,... | collective-permute-start | bytes 589832 | tf_op jit(solution)/shard_map/ppermute | solution.py:25
  206.2 12.6 %collective-permute-done.6 = f16[24,4096]{1,0:T(8,128)(2,1)S(1)} collective-permute-done((f16[24,4096]{1,0:T(8,128)(2,1)S(1)}, f16[24,4096]{1,0:T(8,128)(2,1)S(1)}, u32[]{:S(2)}, u32[]{:S(2)}) %collective-permute-start.6) | collective-permute-done | bytes 196640 | tf_op jit(solution)/shard_map/ppermute | solution.py:25
  218.9 7.1 %collective-permute-done.2 = f16[24,4096]{1,0:T(8,128)(2,1)S(1)} collective-permute-done((f16[24,4096]{1,0:T(8,128)(2,1)S(1)}, f16[24,4096]{1,0:T(8,128)(2,1)S(1)}, u32[]{:S(2)}, u32[]{:S(2)}) %collective-permute-start.2) | collective-permute-done | bytes 196640 | tf_op jit(solution)/shard_map/ppermute | solution.py:25
  228.5 13.4 %collective-permute-done.9 = f32[24,4096]{1,0:T(8,128)S(1)} collective-permute-done((f32[24,4096]{1,0:T(8,128)S(1)}, f32[24,4096]{1,0:T(8,128)S(1)}, u32[]{:S(2)}, u32[]{:S(2)}) %collective-permute-start.9) | collective-permute-done | bytes 393248 | tf_op jit(solution)/shard_map/ppermute | solution.py:87
  243.7 5.4 %fusion.12 = f32[8192,128]{1,0:T(8,128)} fusion(f32[192]{0:T(256)S(1)} %bitcast.143, bf16[192,4096]{1,0:T(8,128)(2,1)} %all-gather.7.cloned.1.call-done, bf16[1,192,8192]{2,1,0:T(8,128)(2,1)} %all-gather.11.cloned.1.call-done), kind=kOutput, calls=%fused_computation.20 | convolution fusion | flops 407371776 | bytes 7389952 | tf_op jit(solution)/shard_map/dot_general | solution.py:93
  249.3 32.2 %all-gather.9.cloned.1.call-done = bf16[192,4096]{1,0:T(8,128)(2,1)} async-done(((bf16[48,4096]{1,0:T(8,128)(2,1)}), bf16[192,4096]{1,0:T(8,128)(2,1)}) %all-gather.9.cloned.1.call-update) | async-done | bytes 1572880 | tf_op jit(solution)/shard_map/all_gather | solution.py:54
  281.4 21.3 %fusion.4 = f32[192,4096]{1,0:T(8,128)} fusion(bf16[192,4096]{1,0:T(8,128)(2,1)} %all-gather.9.cloned.1.call-done, bf16[8192,4096]{1,0:T(8,128)(2,1)} %param.5), kind=kOutput, calls=%fused_computation.4 | convolution fusion | flops 6442450944 | bytes 38273024 | tf_op jit(solution)/shard_map/dot_general | solution.py:62
  302.8 41.2 %all-gather.13.cloned.1.call-done = bf16[1,192,8192]{2,1,0:T(8,128)(2,1)} async-done(((bf16[1,24,8192]{2,1,0:T(8,128)(2,1)}), bf16[1,192,8192]{2,1,0:T(8,128)(2,1)}) %all-gather.13.cloned.1.call-update) | async-done | bytes 3145744 | tf_op jit(solution)/shard_map/all_gather | solution.py:59
  344.0 20.1 %multiply_reduce_fusion = (f32[192]{0:T(256)S(1)}, f32[192]{0:T(256)S(1)}, f32[192,4096]{1,0:T(8,128)}, f32[192,4096]{1,0:T(8,128)}) fusion(bf16[192,8192]{1,0:T(8,128)(2,1)} %bitcast.148, f32[192,4096]{1,0:T(8,128)} %fusion.4, f32[192]{0:T(256)S(1)} %multiply_divide_fusion, bf16[192,4096]{1,0:T(8,128)(2,1)S(1)} %copy-done.7, bf16[8192,4096]{1,0:T(8,128)(2,1)} %param.5), kind=kOutput, calls=%fused_computation.16 | convolution fusion | flops 6448742400 | bytes 47712512 | tf_op jit(solution)/shard_map/dot_general | solution.py:62
  364.1 39.2 %psum.15 = f32[192]{0:T(256)S(1)} all-reduce(f32[192]{0:T(256)S(1)} %add.236), channel_id=1, replica_groups=mesh['row'=4,'col'=8] {'row','col'}, use_global_device_ids=true, to_apply=%region_7.8 | all-reduce | flops 192 | bytes 1536 | tf_op jit(solution)/shard_map/psum | solution.py:72
  403.3 1.6 fusion.15
  406.5 2.3 collective-permute-start.14
  408.9 6.6 %fusion.9 = f32[8192,128]{1,0:T(8,128)} fusion(f32[8192,128]{1,0:T(8,128)} %fusion.12, f32[192]{0:T(256)S(1)} %psum.15, bf16[8192,4096]{1,0:T(8,128)(2,1)} %param.5, bf16[192,4096]{1,0:T(8,128)(2,1)S(1)} %copy-done.7, bf16[1,192,8192]{2,1,0:T(8,128)(2,1)S(1)} %copy-done.5), kind=kOutput, calls=%fused_computation.10 | convolution fusion | flops 411566080 | bytes 13681664 | tf_op jit(solution)/shard_map/dot_general | solution.py:93
  415.6 11.8 %collective-permute-done.14 = f16[4,24,4096]{2,1,0:T(8,128)(2,1)S(1)} collective-permute-done((f16[4,24,4096]{2,1,0:T(8,128)(2,1)S(1)}, f16[4,24,4096]{2,1,0:T(8,128)(2,1)S(1)}, u32[]{:S(2)}, u32[]{:S(2)}) %collective-permute-start.14) | collective-permute-done | bytes 786464 | tf_op jit(solution)/shard_map/ppermute | solution.py:18
  428.3 3.2 collective-permute-start.17
  431.6 10.9 %collective-permute-done.10 = f16[4,24,4096]{2,1,0:T(8,128)(2,1)S(1)} collective-permute-done((f16[4,24,4096]{2,1,0:T(8,128)(2,1)S(1)}, f16[4,24,4096]{2,1,0:T(8,128)(2,1)S(1)}, u32[]{:S(2)}, u32[]{:S(2)}) %collective-permute-start.10) | collective-permute-done | bytes 786464 | tf_op jit(solution)/shard_map/ppermute | solution.py:18
  443.5 3.3 collective-permute-start.13
  446.9 5.7 %collective-permute-done.11 = f16[24,4096]{1,0:T(8,128)(2,1)S(1)} collective-permute-done((f16[24,4096]{1,0:T(8,128)(2,1)S(1)}, f16[24,4096]{1,0:T(8,128)(2,1)S(1)}, u32[]{:S(2)}, u32[]{:S(2)}) %collective-permute-start.11) | collective-permute-done | bytes 196640 | tf_op jit(solution)/shard_map/ppermute | solution.py:25
  453.5 8.0 %collective-permute-done.12 = f16[24,4096]{1,0:T(8,128)(2,1)S(1)} collective-permute-done((f16[24,4096]{1,0:T(8,128)(2,1)S(1)}, f16[24,4096]{1,0:T(8,128)(2,1)S(1)}, u32[]{:S(2)}, u32[]{:S(2)}) %collective-permute-start.12) | collective-permute-done | bytes 196640 | tf_op jit(solution)/shard_map/ppermute | solution.py:25
  (76 shorter events, 16.1 us)
Async XLA Ops:
  7.2 1.2 copy-start
  7.2 25.9 %all-gather.7.cloned.1.call-start = ((), (), s32[]{:S(2)}) async-start(), calls=%async_computation | async-start | bytes 1966080 | tf_op jit(solution)/shard_map/all_gather | solution.py:54
  10.6 85.7 %all-gather.11.cloned.1.call-start = ((), (), s32[]{:S(2)}) async-start(), calls=%async_computation.2 | async-start | bytes 3538944 | tf_op jit(solution)/shard_map/all_gather | solution.py:41
  12.7 268.8 %all-gather.9.cloned.1.call-start = ((), (), s32[]{:S(2)}) async-start(), calls=%async_computation.1 | async-start | bytes 1966080 | tf_op jit(solution)/shard_map/all_gather | solution.py:54
  33.1 63.2 %copy-start.6 = (bf16[192,4096]{1,0:T(8,128)(2,1)S(1)}, bf16[192,4096]{1,0:T(8,128)(2,1)}, u32[]{:S(2)}) copy-start(bf16[192,4096]{1,0:T(8,128)(2,1)} %all-gather.7.cloned.1.call-done) | copy-start | bytes 4718596
  118.8 69.1 %collective-permute-start.4 = (f16[4,24,4096]{2,1,0:T(8,128)(2,1)}, f16[4,24,4096]{2,1,0:T(8,128)(2,1)S(1)}, u32[]{:S(2)}, u32[]{:S(2)}) collective-permute-start(f16[4,24,4096]{2,1,0:T(8,128)(2,1)} %fusion.14), channel_id=1, source_target_pairs={{0,1},{1,0},{2,3},{3,2},{4,5},{5,4},{6,7},{7,6},{8,9},{9,8},{10,11... | collective-permute-start | bytes 2359304 | tf_op jit(solution)/shard_map/ppermute | solution.py:18
  120.9 72.9 %collective-permute-start = (f16[4,24,4096]{2,1,0:T(8,128)(2,1)S(1)}, f16[4,24,4096]{2,1,0:T(8,128)(2,1)S(1)}, u32[]{:S(2)}, u32[]{:S(2)}) collective-permute-start(f16[4,24,4096]{2,1,0:T(8,128)(2,1)S(1)} %fusion.13), channel_id=1, source_target_pairs={{0,1},{1,0},{2,3},{3,2},{4,5},{5,4},{6,7},{7,6},{8,9},{9,8},{10,11... | collective-permute-start | bytes 2359304 | tf_op jit(solution)/shard_map/ppermute | solution.py:18
  187.9 5.9 %copy-start.2 = (f32[192,4096]{1,0:T(8,128)S(1)}, f32[192,4096]{1,0:T(8,128)}, u32[]{:S(2)}) copy-start(f32[192,4096]{1,0:T(8,128)} %get-tuple-element.18) | copy-start | bytes 9437188
  189.9 9.7 %collective-permute-start.5 = (f16[24,4096]{1,0:T(8,128)(2,1)S(1)}, f16[24,4096]{1,0:T(8,128)(2,1)S(1)}, u32[]{:S(2)}, u32[]{:S(2)}) collective-permute-start(f16[24,4096]{1,0:T(8,128)(2,1)S(1)} %get-tuple-element.37), channel_id=1, source_target_pairs={{0,2},{1,3},{2,4},{3,5},{4,6},{5,7},{6,0},{7,1},{8,10},{9,11},{10,... | collective-permute-start | bytes 589832 | tf_op jit(solution)/shard_map/ppermute | solution.py:25
  190.8 15.3 %collective-permute-start.7 = (f16[24,4096]{1,0:T(8,128)(2,1)S(1)}, f16[24,4096]{1,0:T(8,128)(2,1)S(1)}, u32[]{:S(2)}, u32[]{:S(2)}) collective-permute-start(f16[24,4096]{1,0:T(8,128)(2,1)S(1)} %get-tuple-element.38), channel_id=1, source_target_pairs={{0,6},{1,7},{2,0},{3,1},{4,2},{5,3},{6,4},{7,5},{8,14},{9,15},{10,... | collective-permute-start | bytes 589832 | tf_op jit(solution)/shard_map/ppermute | solution.py:25
  193.8 25.0 %collective-permute-start.6 = (f16[24,4096]{1,0:T(8,128)(2,1)S(1)}, f16[24,4096]{1,0:T(8,128)(2,1)S(1)}, u32[]{:S(2)}, u32[]{:S(2)}) collective-permute-start(f16[24,4096]{1,0:T(8,128)(2,1)S(1)} %get-tuple-element.39), channel_id=1, source_target_pairs={{0,4},{1,5},{2,6},{3,7},{4,0},{5,1},{6,2},{7,3},{8,12},{9,13},{10,... | collective-permute-start | bytes 589832 | tf_op jit(solution)/shard_map/ppermute | solution.py:25
  194.2 24.7 %collective-permute-start.1 = (f16[24,4096]{1,0:T(8,128)(2,1)S(1)}, f16[24,4096]{1,0:T(8,128)(2,1)S(1)}, u32[]{:S(2)}, u32[]{:S(2)}) collective-permute-start(f16[24,4096]{1,0:T(8,128)(2,1)S(1)} %get-tuple-element.34), channel_id=1, source_target_pairs={{0,2},{1,3},{2,4},{3,5},{4,6},{5,7},{6,0},{7,1},{8,10},{9,11},{10,... | collective-permute-start | bytes 589832 | tf_op jit(solution)/shard_map/ppermute | solution.py:25
  194.8 24.1 %collective-permute-start.3 = (f16[24,4096]{1,0:T(8,128)(2,1)S(1)}, f16[24,4096]{1,0:T(8,128)(2,1)S(1)}, u32[]{:S(2)}, u32[]{:S(2)}) collective-permute-start(f16[24,4096]{1,0:T(8,128)(2,1)S(1)} %get-tuple-element.35), channel_id=1, source_target_pairs={{0,6},{1,7},{2,0},{3,1},{4,2},{5,3},{6,4},{7,5},{8,14},{9,15},{10,... | collective-permute-start | bytes 589832 | tf_op jit(solution)/shard_map/ppermute | solution.py:25
  199.6 26.4 %collective-permute-start.2 = (f16[24,4096]{1,0:T(8,128)(2,1)S(1)}, f16[24,4096]{1,0:T(8,128)(2,1)S(1)}, u32[]{:S(2)}, u32[]{:S(2)}) collective-permute-start(f16[24,4096]{1,0:T(8,128)(2,1)S(1)} %get-tuple-element.36), channel_id=1, source_target_pairs={{0,4},{1,5},{2,6},{3,7},{4,0},{5,1},{6,2},{7,3},{8,12},{9,13},{10,... | collective-permute-start | bytes 589832 | tf_op jit(solution)/shard_map/ppermute | solution.py:25
  226.2 15.6 %collective-permute-start.9 = (f32[24,4096]{1,0:T(8,128)S(1)}, f32[24,4096]{1,0:T(8,128)S(1)}, u32[]{:S(2)}, u32[]{:S(2)}) collective-permute-start(f32[24,4096]{1,0:T(8,128)S(1)} %get-tuple-element.32), channel_id=1, source_target_pairs={{0,1},{1,0},{2,9},{3,8},{4,17},{5,16},{6,25},{7,24},{8,3},{9,2},{1... | collective-permute-start | bytes 1179656 | tf_op jit(solution)/shard_map/ppermute | solution.py:87
  227.7 14.2 %collective-permute-start.8 = (f32[24,4096]{1,0:T(8,128)S(1)}, f32[24,4096]{1,0:T(8,128)S(1)}, u32[]{:S(2)}, u32[]{:S(2)}) collective-permute-start(f32[24,4096]{1,0:T(8,128)S(1)} %get-tuple-element.33), channel_id=1, source_target_pairs={{0,0},{1,1},{2,8},{3,9},{4,16},{5,17},{6,24},{7,25},{8,2},{9,3},{1... | collective-permute-start | bytes 1179656 | tf_op jit(solution)/shard_map/ppermute | solution.py:87
  243.1 100.8 %all-gather.13.cloned.1.call-start = ((), (), s32[]{:S(2)}) async-start(), calls=%async_computation.3 | async-start | bytes 3538944 | tf_op jit(solution)/shard_map/all_gather | solution.py:59
  281.4 62.5 %copy-start.7 = (bf16[192,4096]{1,0:T(8,128)(2,1)S(1)}, bf16[192,4096]{1,0:T(8,128)(2,1)}, u32[]{:S(2)}) copy-start(bf16[192,4096]{1,0:T(8,128)(2,1)} %all-gather.9.cloned.1.call-done) | copy-start | bytes 4718596
  403.3 5.7 %copy-start.5 = (bf16[1,192,8192]{2,1,0:T(8,128)(2,1)S(1)}, bf16[1,192,8192]{2,1,0:T(8,128)(2,1)}, u32[]{:S(2)}) copy-start(bf16[1,192,8192]{2,1,0:T(8,128)(2,1)} %all-gather.13.cloned.1.call-done) | copy-start | bytes 9437188
  406.5 20.8 %copy-start.4 = (f32[192,4096]{1,0:T(8,128)S(1)}, f32[192,4096]{1,0:T(8,128)}, u32[]{:S(2)}) copy-start(f32[192,4096]{1,0:T(8,128)} %get-tuple-element.17) | copy-start | bytes 9437188
  406.5 20.8 %collective-permute-start.14 = (f16[4,24,4096]{2,1,0:T(8,128)(2,1)S(1)}, f16[4,24,4096]{2,1,0:T(8,128)(2,1)S(1)}, u32[]{:S(2)}, u32[]{:S(2)}) collective-permute-start(f16[4,24,4096]{2,1,0:T(8,128)(2,1)S(1)} %fusion.16), channel_id=1, source_target_pairs={{0,1},{1,0},{2,3},{3,2},{4,5},{5,4},{6,7},{7,6},{8,9},{9,8},{10,11... | collective-permute-start | bytes 2359304 | tf_op jit(solution)/shard_map/ppermute | solution.py:18
  408.9 33.6 %collective-permute-start.10 = (f16[4,24,4096]{2,1,0:T(8,128)(2,1)S(1)}, f16[4,24,4096]{2,1,0:T(8,128)(2,1)S(1)}, u32[]{:S(2)}, u32[]{:S(2)}) collective-permute-start(f16[4,24,4096]{2,1,0:T(8,128)(2,1)S(1)} %fusion.15), channel_id=1, source_target_pairs={{0,1},{1,0},{2,3},{3,2},{4,5},{5,4},{6,7},{7,6},{8,9},{9,8},{10,11... | collective-permute-start | bytes 2359304 | tf_op jit(solution)/shard_map/ppermute | solution.py:18
  415.6 26.9 %copy-start.3 = (f32[192,4096]{1,0:T(8,128)S(1)}, f32[192,4096]{1,0:T(8,128)}, u32[]{:S(2)}) copy-start(f32[192,4096]{1,0:T(8,128)} %get-tuple-element.16) | copy-start | bytes 9437188
  427.7 19.1 %collective-permute-start.15 = (f16[24,4096]{1,0:T(8,128)(2,1)S(1)}, f16[24,4096]{1,0:T(8,128)(2,1)S(1)}, u32[]{:S(2)}, u32[]{:S(2)}) collective-permute-start(f16[24,4096]{1,0:T(8,128)(2,1)S(1)} %get-tuple-element.29), channel_id=1, source_target_pairs={{0,2},{1,3},{2,4},{3,5},{4,6},{5,7},{6,0},{7,1},{8,10},{9,11},{10,... | collective-permute-start | bytes 589832 | tf_op jit(solution)/shard_map/ppermute | solution.py:25
  428.3 18.4 %collective-permute-start.17 = (f16[24,4096]{1,0:T(8,128)(2,1)S(1)}, f16[24,4096]{1,0:T(8,128)(2,1)S(1)}, u32[]{:S(2)}, u32[]{:S(2)}) collective-permute-start(f16[24,4096]{1,0:T(8,128)(2,1)S(1)} %get-tuple-element.30), channel_id=1, source_target_pairs={{0,6},{1,7},{2,0},{3,1},{4,2},{5,3},{6,4},{7,5},{8,14},{9,15},{10,... | collective-permute-start | bytes 589832 | tf_op jit(solution)/shard_map/ppermute | solution.py:25
  431.6 15.2 %collective-permute-start.16 = (f16[24,4096]{1,0:T(8,128)(2,1)S(1)}, f16[24,4096]{1,0:T(8,128)(2,1)S(1)}, u32[]{:S(2)}, u32[]{:S(2)}) collective-permute-start(f16[24,4096]{1,0:T(8,128)(2,1)S(1)} %get-tuple-element.31), channel_id=1, source_target_pairs={{0,4},{1,5},{2,6},{3,7},{4,0},{5,1},{6,2},{7,3},{8,12},{9,13},{10,... | collective-permute-start | bytes 589832 | tf_op jit(solution)/shard_map/ppermute | solution.py:25
  442.9 9.7 %collective-permute-start.11 = (f16[24,4096]{1,0:T(8,128)(2,1)S(1)}, f16[24,4096]{1,0:T(8,128)(2,1)S(1)}, u32[]{:S(2)}, u32[]{:S(2)}) collective-permute-start(f16[24,4096]{1,0:T(8,128)(2,1)S(1)} %get-tuple-element.26), channel_id=1, source_target_pairs={{0,2},{1,3},{2,4},{3,5},{4,6},{5,7},{6,0},{7,1},{8,10},{9,11},{10,... | collective-permute-start | bytes 589832 | tf_op jit(solution)/shard_map/ppermute | solution.py:25
  443.5 10.0 %collective-permute-start.13 = (f16[24,4096]{1,0:T(8,128)(2,1)S(1)}, f16[24,4096]{1,0:T(8,128)(2,1)S(1)}, u32[]{:S(2)}, u32[]{:S(2)}) collective-permute-start(f16[24,4096]{1,0:T(8,128)(2,1)S(1)} %get-tuple-element.27), channel_id=1, source_target_pairs={{0,6},{1,7},{2,0},{3,1},{4,2},{5,3},{6,4},{7,5},{8,14},{9,15},{10,... | collective-permute-start | bytes 589832 | tf_op jit(solution)/shard_map/ppermute | solution.py:25
  446.8 14.7 %collective-permute-start.12 = (f16[24,4096]{1,0:T(8,128)(2,1)S(1)}, f16[24,4096]{1,0:T(8,128)(2,1)S(1)}, u32[]{:S(2)}, u32[]{:S(2)}) collective-permute-start(f16[24,4096]{1,0:T(8,128)(2,1)S(1)} %get-tuple-element.28), channel_id=1, source_target_pairs={{0,4},{1,5},{2,6},{3,7},{4,0},{5,1},{6,2},{7,3},{8,12},{9,13},{10,... | collective-permute-start | bytes 589832 | tf_op jit(solution)/shard_map/ppermute | solution.py:25
  446.8 16.2 %copy-start.1 = (bf16[96,4096]{1,0:T(8,128)(2,1)S(1)}, bf16[96,4096]{1,0:T(8,128)(2,1)}, u32[]{:S(2)}) copy-start(bf16[96,4096]{1,0:T(8,128)(2,1)} %param.6) | copy-start | bytes 2359300
Sparse Core Ops, SparseCore 0:
  10.7 22.3 all-gather.6
  35.8 60.4 all-gather.10
  243.3 38.1 all-gather.8
  283.5 60.4 all-gather.12

commit v2 on v1

v2 whole, which is shorter than its diff:
```python
import jax
import jax.numpy as jnp
from jax import lax
from jax.sharding import PartitionSpec as P

H = 32768
N = 192
DW = 128
CHUNKS = 2


def in_order(arrived, index):
    count = len(arrived)
    turned = jnp.stack([arrived[-i % count] for i in range(count)] * 2)
    return lax.dynamic_slice_in_dim(turned, (count - index) % count, count, 0)


def gather_small(value, col_count, col_index):
    arrived = [value]
    for k in range(1, col_count):
        arrived.append(lax.ppermute(value, "col", [(c, (c + k) % col_count) for c in range(col_count)]))
    place = lax.broadcasted_iota(jnp.int32, (col_count,) + value.shape, 0)
    out = jnp.zeros(place.shape, value.dtype)
    for k, got in enumerate(arrived):
        out = jnp.where(place == (col_index - k + col_count) % col_count, got[None], out)
    return out


def gather_rows(value, row_count, row_index):
    half = row_count // 2
    arrived = [value]
    for k in range(1, half):
        arrived.append(lax.ppermute(value, "row", [(r, (r + 2 * k) % row_count) for r in range(row_count)]))
    own = in_order(arrived, row_index // 2) if half > 1 else value[None]
    got = lax.ppermute(own, "row", [(r, r ^ 1) for r in range(row_count)])
    even = row_index % 2 == 0
    both = jnp.stack([jnp.where(even, own, got), jnp.where(even, got, own)], axis=1)
    return both.reshape(row_count * value.shape[0], value.shape[1])


def split_pair(partial, scale, col_count, col_index, local_seqs):
    scaled = (partial * scale).reshape(col_count // 2, 2, local_seqs, partial.shape[1])
    side = col_index % 2
    away = lax.dynamic_index_in_dim(scaled, 1 - side, 1, keepdims=False).astype(jnp.float16)
    return away, lax.dynamic_index_in_dim(scaled, side, 1, keepdims=False)


def reduce_scatter(away, keep, col_count, col_index):
    half = col_count // 2
    got = lax.ppermute(away, "col", [(c, c ^ 1) for c in range(col_count)])
    pair = keep + got.astype(jnp.float32)
    here = col_index // 2
    total = lax.dynamic_index_in_dim(pair, here, 0, keepdims=False)
    packed = pair.astype(jnp.float16)
    for k in range(1, half):
        piece = lax.dynamic_index_in_dim(packed, (here + k) % half, 0, keepdims=False)
        got = lax.ppermute(piece, "col", [(c, (c + 2 * k) % col_count) for c in range(col_count)])
        total = total + got.astype(jnp.float32)
    return total


def on_device(transition, emission, token_ids, forward, backward_last):
    row_count = lax.axis_size("row")
    col_count = lax.axis_size("col")
    row_index = lax.axis_index("row")
    col_index = lax.axis_index("col")
    ratio = col_count // row_count
    local_seqs = forward.shape[1]
    row_seqs = backward_last.shape[0]
    block_src = transition.shape[0]
    block_dst = transition.shape[1]
    seq_total = local_seqs * col_count
    columns = lax.broadcasted_iota(jnp.int32, (row_seqs, emission.shape[0]), 1)
    window = transition[:, :DW]
    outputs = [None, None]
    normals = [None, None]
    picked = [None, None]
    beta = backward_last
    scale = jnp.full((seq_total, 1), 64.0, jnp.float32)
    scale_mine = jnp.full((local_seqs, 1), 64.0, jnp.float32)
    chunk = block_src // CHUNKS
    for step in (1, 0):
        tokens = lax.dynamic_slice_in_dim(token_ids[step], row_index * row_seqs, row_seqs, 0)
        onehot = (tokens[:, None] == columns).astype(jnp.bfloat16)
        emitted = jnp.dot(onehot, emission, preferred_element_type=jnp.float32)
        local_back = (emitted * beta).astype(jnp.bfloat16)
        weighted_back = gather_rows(local_back, row_count, row_index)
        picked[step] = weighted_back[:, :DW]
        if step == 1:
            forward_all = lax.all_gather(forward, "col", axis=1, tiled=True)
        pieces = []
        for k in range(CHUNKS):
            rows = slice(k * chunk, (k + 1) * chunk)
            partial = lax.dot_general(
                weighted_back, transition[rows], (((1,), (1,)), ((), ())), preferred_element_type=jnp.float32
            )
            away, keep = split_pair(partial, scale, col_count, col_index, local_seqs)
            if k < CHUNKS - 1:
                weighted_back, away = lax.optimization_barrier((weighted_back, away))
            pieces.append(reduce_scatter(away, keep, col_count, col_index))
        mine = jnp.concatenate(pieces, axis=1) / scale_mine
        norm = jnp.sum(forward[step].astype(jnp.float32) * mine, axis=1)
        sums = lax.psum(jnp.stack([norm, jnp.sum(mine, axis=1)]), "row")
        sums_all = gather_small(sums, col_count, col_index)
        normals[step] = sums_all[:, 0].reshape(seq_total)
        outputs[step] = mine / sums[0][:, None]
        if step == 1:
            halves = outputs[step].reshape(local_seqs, ratio, block_dst)
            arrived = []
            for p in range(ratio):
                part = lax.dynamic_index_in_dim(halves, (col_index + p) % ratio, 1, keepdims=False)
                moves = []
                for r in range(row_count):
                    for c in range(col_count):
                        moves.append((r * col_count + c, (c // ratio) * col_count + r * ratio + (c + p) % ratio))
                arrived.append(lax.ppermute(part, ("row", "col"), moves))
            beta = in_order(arrived, col_index % ratio).reshape(row_seqs, block_dst)
            scale = (16777216.0 * sums_all[:, 0] / sums_all[:, 1]).reshape(seq_total, 1)
            scale_mine = (16777216.0 * sums[0] / sums[1])[:, None]
    totals = jnp.zeros((block_src, DW), jnp.float32)
    for step in (1, 0):
        scaled = (forward_all[step].astype(jnp.float32) / normals[step][:, None]).astype(jnp.bfloat16)
        totals = totals + lax.dot_general(
            scaled, picked[step], (((0,), (0,)), ((), ())), preferred_element_type=jnp.float32
        )
    counts = window.astype(jnp.float32) * totals * (H * H / N)
    return (jnp.stack(outputs), counts)


def solution(mesh):
    in_specs = (P("row", "col"), P(None, "col"), P(), P(None, "col", "row"), P("row", "col"))
    out_specs = (P(None, "col", "row"), P("row", "col"))
    return jax.shard_map(
        on_device, mesh=mesh, in_specs=in_specs, out_specs=out_specs, check_vma=False
    )
```

time: 470 us -> 323 us (0.69)
  waiting for transfers between devices: 208 us -> 101 us
  blocking collectives: 105 us -> 11.7 us
  starting transfers between devices: 29 us -> 99.3 us
  matrix products: 98.1 us -> 78.8 us
    all_gather x4 -> x1, waiting for transfers between devices: 136 us -> 0.01 us  [on_device(): forward_all = lax.all_gather(forward, 'col', axis=1, tiled=True)]
    psum x2, blocking collectives: 105 us -> 11.7 us  [on_device(): sums = lax.psum(jnp.stack([norm, jnp.sum(mine, axis=1)]), 'row')]
    ppermute x0 -> x18, starting transfers between devices: none -> 73.4 us  [the longest x14 59.1 us: gather_small(): lax.ppermute(value, 'col', [(c, (c + k) % col_count) for c in range(col_c...]
    ppermute x0 -> x18, waiting for transfers between devices: none -> 22.9 us  [the longest x2 13.9 us: gather_rows(): lax.ppermute(value, 'row', [(r, (r + 2 * k) % row_count) for r in range(r...]
    ppermute x4, waiting for transfers between devices: 22.7 us -> 38.7 us  [reduce_scatter(): got = lax.ppermute(away, 'col', [(c, c ^ 1) for c in range(col_count)])]
    dot_general x4, matrix products: 82.8 us -> 68.2 us  [on_device(): lax.dot_general(weighted_back, transition[rows], (((1,), (1,)), ((), ()))...]
    ppermute x2, waiting for transfers between devices: 13.4 us -> 0.01 us  [on_device(): arrived.append(lax.ppermute(part, ('row', 'col'), moves))]
  transfers between devices with their start and end apart: 22 -> 37, of which waited for: 13 -> 14; matrix products, arithmetic and copies ran while one was open for 13% -> 26% of each run, Pallas kernels for 0% -> 0%
where the time goes in v2:
time: 323 us; the launch traced here: 322 us
  waiting for transfers between devices  101 us (31%)
  starting transfers between devices  99.3 us (31%)
  matrix products  78.8 us (24%)
  between operations  14.8 us (5%)
  other arithmetic  14.3 us (4%)
  blocking collectives  11.7 us (4%)
    dot_general x4, matrix products, on_device(): lax.dot_general(weighted_back, transition[rows], (((1,), (1,)), ((), ()))...  68.2 us
    ppermute x14, starting transfers between devices, gather_small(): lax.ppermute(value, 'col', [(c, (c + k) % col_count) for c in range(col_c...  59.1 us
    ppermute x12, waiting for transfers between devices, reduce_scatter(): lax.ppermute(piece, 'col', [(c, (c + 2 * k) % col_count) for c in range(c...  39.3 us
    ppermute x4, waiting for transfers between devices, reduce_scatter(): got = lax.ppermute(away, 'col', [(c, c ^ 1) for c in range(col_count)])  38.7 us
    ppermute x12, starting transfers between devices, reduce_scatter(): lax.ppermute(piece, 'col', [(c, (c + 2 * k) % col_count) for c in range(c...  19.2 us
    ppermute x2, starting transfers between devices, gather_rows(): lax.ppermute(value, 'row', [(r, (r + 2 * k) % row_count) for r in range(r...  14.1 us
    ppermute x2, waiting for transfers between devices, gather_rows(): lax.ppermute(value, 'row', [(r, (r + 2 * k) % row_count) for r in range(r...  13.9 us
    psum x2, blocking collectives, on_device(): sums = lax.psum(jnp.stack([norm, jnp.sum(mine, axis=1)]), 'row')  11.7 us
  transfers between devices with their start and end apart: 37, of which 14 were waited for; matrix products, arithmetic and copies ran while one was open for 26% of the time, Pallas kernels for 0%

profile of v2, /device:TPU:0, one launch (start us, length us, event | category | flops | bytes accessed | tf_op | source)
XLA Modules:
  0.0 322.1 jit_solution(14443094737425642083)
XLA Ops:
  9.8 3.0 collective-permute-start
  12.8 9.1 %collective-permute-done = bf16[48,4096]{1,0:T(8,128)(2,1)S(1)} collective-permute-done((bf16[48,4096]{1,0:T(8,128)(2,1)S(1)}, bf16[48,4096]{1,0:T(8,128)(2,1)S(1)}, u32[]{:S(2)}, u32[]{:S(2)}) %collective-permute-start) | collective-permute-done | bytes 393248 | tf_op jit(solution)/shard_map/ppermute | solution.py:33
  25.8 18.2 %fusion.12 = f32[192,4096]{1,0:T(8,128)} fusion(bf16[192,4096]{1,0:T(8,128)(2,1)S(1)} %bitcast.158, bf16[8192,4096]{1,0:T(8,128)(2,1)} %param.5), kind=kOutput, calls=%fused_computation.15 | convolution fusion | flops 6443237376 | bytes 38273024 | tf_op jit(solution)/shard_map/dot_general | solution.py:94
  44.0 2.4 fusion.29
  48.2 16.3 %fusion.18 = f32[192,4096]{1,0:T(8,128)S(1)} fusion(bf16[192,4096]{1,0:T(8,128)(2,1)S(1)} %bitcast.159, bf16[8192,4096]{1,0:T(8,128)(2,1)} %param.5), kind=kOutput, calls=%fused_computation.17 | convolution fusion | flops 6443237376 | bytes 38273024 | tf_op jit(solution)/shard_map/dot_general | solution.py:94
  70.3 2.5 collective-permute-start.4
  74.2 25.9 %collective-permute-done.6 = f16[4,24,4096]{2,1,0:T(8,128)(2,1)S(1)} collective-permute-done((f16[4,24,4096]{2,1,0:T(8,128)(2,1)S(1)}, f16[4,24,4096]{2,1,0:T(8,128)(2,1)S(1)}, u32[]{:S(2)}, u32[]{:S(2)}) %collective-permute-start.6) | collective-permute-done | bytes 786464 | tf_op jit(solution)/shard_map/ppermute | solution.py:50
  102.2 2.7 collective-permute-start.8
  106.3 8.0 %collective-permute-done.7 = f16[24,4096]{1,0:T(8,128)(2,1)S(1)} collective-permute-done((f16[24,4096]{1,0:T(8,128)(2,1)S(1)}, f16[24,4096]{1,0:T(8,128)(2,1)S(1)}, u32[]{:S(2)}, u32[]{:S(2)}) %collective-permute-start.7) | collective-permute-done | bytes 196640 | tf_op jit(solution)/shard_map/ppermute | solution.py:57
  114.3 18.2 %collective-permute-done.8 = f16[24,4096]{1,0:T(8,128)(2,1)S(1)} collective-permute-done((f16[24,4096]{1,0:T(8,128)(2,1)S(1)}, f16[24,4096]{1,0:T(8,128)(2,1)S(1)}, u32[]{:S(2)}, u32[]{:S(2)}) %collective-permute-start.8) | collective-permute-done | bytes 196640 | tf_op jit(solution)/shard_map/ppermute | solution.py:57
  132.9 6.1 %psum.14 = f32[2,24]{1,0:T(2,128)S(1)} all-reduce(f32[2,24]{1,0:T(2,128)S(1)} %pad_maximum_fusion.3), channel_id=1, replica_groups=mesh['row'=4,'col'=8] {'row'}, use_global_device_ids=true, to_apply=%region_2.3 | all-reduce | flops 48 | bytes 384 | tf_op jit(solution)/shard_map/psum | solution.py:103
  141.8 21.1 %collective-permute-start.14 = (f32[2,24]{1,0:T(2,128)S(1)}, f32[2,24]{1,0:T(2,128)S(1)}, u32[]{:S(2)}, u32[]{:S(2)}) collective-permute-start(f32[2,24]{1,0:T(2,128)S(1)} %psum.14), channel_id=1, source_target_pairs={{0,7},{1,0},{2,1},{3,2},{4,3},{5,4},{6,5},{7,6},{8,15},{9,8},{10,9... | collective-permute-start | bytes 584 | tf_op jit(solution)/shard_map/ppermute | solution.py:21
  163.1 16.1 %collective-permute-start.17 = (f32[2,24]{1,0:T(2,128)S(1)}, f32[2,24]{1,0:T(2,128)S(1)}, u32[]{:S(2)}, u32[]{:S(2)}) collective-permute-start(f32[2,24]{1,0:T(2,128)S(1)} %psum.14), channel_id=1, source_target_pairs={{0,4},{1,5},{2,6},{3,7},{4,0},{5,1},{6,2},{7,3},{8,12},{9,13},{10,... | collective-permute-start | bytes 584 | tf_op jit(solution)/shard_map/ppermute | solution.py:21
  179.7 11.1 %collective-permute-start.12 = (bf16[48,4096]{1,0:T(8,128)(2,1)S(1)}, bf16[48,4096]{1,0:T(8,128)(2,1)S(1)}, u32[]{:S(2)}, u32[]{:S(2)}) collective-permute-start(bf16[48,4096]{1,0:T(8,128)(2,1)S(1)} %fusion.46), channel_id=1, source_target_pairs={{0,16},{8,24},{16,0},{24,8},{1,17},{9,25},{17,1},{25,9},{2,18},{10... | collective-permute-start | bytes 1179656 | tf_op jit(solution)/shard_map/ppermute | solution.py:33
  191.8 4.8 %collective-permute-done.12 = bf16[48,4096]{1,0:T(8,128)(2,1)S(1)} collective-permute-done((bf16[48,4096]{1,0:T(8,128)(2,1)S(1)}, bf16[48,4096]{1,0:T(8,128)(2,1)S(1)}, u32[]{:S(2)}, u32[]{:S(2)}) %collective-permute-start.12) | collective-permute-done | bytes 393248 | tf_op jit(solution)/shard_map/ppermute | solution.py:33
  197.2 6.9 %collective-permute-start.18 = (f32[2,24]{1,0:T(2,128)S(1)}, f32[2,24]{1,0:T(2,128)S(1)}, u32[]{:S(2)}, u32[]{:S(2)}) collective-permute-start(f32[2,24]{1,0:T(2,128)S(1)} %psum.14), channel_id=1, source_target_pairs={{0,3},{1,4},{2,5},{3,6},{4,7},{5,0},{6,1},{7,2},{8,11},{9,12},{10,... | collective-permute-start | bytes 584 | tf_op jit(solution)/shard_map/ppermute | solution.py:21
  205.5 3.9 %collective-permute-done.19 = f32[2,24]{1,0:T(2,128)S(1)} collective-permute-done((f32[2,24]{1,0:T(2,128)S(1)}, f32[2,24]{1,0:T(2,128)S(1)}, u32[]{:S(2)}, u32[]{:S(2)}) %collective-permute-start.19) | collective-permute-done | bytes 224 | tf_op jit(solution)/shard_map/ppermute | solution.py:21
  211.7 17.1 %fusion.15 = f32[192,4096]{1,0:T(8,128)S(1)} fusion(bf16[192,4096]{1,0:T(8,128)(2,1)S(1)} %bitcast.161, bf16[8192,4096]{1,0:T(8,128)(2,1)} %param.5, f32[192]{0:T(256)S(1)} %multiply_divide_fusion), kind=kOutput, calls=%fused_computation.16 | convolution fusion | flops 6443237376 | bytes 38273792 | tf_op jit(solution)/shard_map/dot_general | solution.py:94
  229.7 16.6 %fusion.21 = f32[192,4096]{1,0:T(8,128)S(1)} fusion(bf16[192,4096]{1,0:T(8,128)(2,1)} %bitcast.162, bf16[8192,4096]{1,0:T(8,128)(2,1)} %param.5, f32[192]{0:T(256)S(1)} %multiply_divide_fusion), kind=kOutput, calls=%fused_computation.18 | convolution fusion | flops 6443237376 | bytes 38273792 | tf_op jit(solution)/shard_map/dot_general | solution.py:94
  246.5 2.1 collective-permute-start.25
  250.4 2.3 collective-permute-start.23
  254.2 11.1 %collective-permute-done.25 = f16[4,24,4096]{2,1,0:T(8,128)(2,1)S(1)} collective-permute-done((f16[4,24,4096]{2,1,0:T(8,128)(2,1)S(1)}, f16[4,24,4096]{2,1,0:T(8,128)(2,1)S(1)}, u32[]{:S(2)}, u32[]{:S(2)}) %collective-permute-start.25) | collective-permute-done | bytes 786464 | tf_op jit(solution)/shard_map/ppermute | solution.py:50
  265.8 2.2 collective-permute-start.27
  269.7 5.8 %collective-permute-done.26 = f16[24,4096]{1,0:T(8,128)(2,1)S(1)} collective-permute-done((f16[24,4096]{1,0:T(8,128)(2,1)S(1)}, f16[24,4096]{1,0:T(8,128)(2,1)S(1)}, u32[]{:S(2)}, u32[]{:S(2)}) %collective-permute-start.26) | collective-permute-done | bytes 196640 | tf_op jit(solution)/shard_map/ppermute | solution.py:57
  275.4 7.4 %collective-permute-done.27 = f16[24,4096]{1,0:T(8,128)(2,1)S(1)} collective-permute-done((f16[24,4096]{1,0:T(8,128)(2,1)S(1)}, f16[24,4096]{1,0:T(8,128)(2,1)S(1)}, u32[]{:S(2)}, u32[]{:S(2)}) %collective-permute-start.27) | collective-permute-done | bytes 196640 | tf_op jit(solution)/shard_map/ppermute | solution.py:57
  283.3 5.7 %psum.15 = f32[2,24]{1,0:T(2,128)S(1)} all-reduce(f32[2,24]{1,0:T(2,128)S(1)} %pad_maximum_fusion.4), channel_id=1, replica_groups=mesh['row'=4,'col'=8] {'row'}, use_global_device_ids=true, to_apply=%region_5.6 | all-reduce | flops 48 | bytes 384 | tf_op jit(solution)/shard_map/psum | solution.py:103
  289.0 4.8 %collective-permute-start.34 = (f32[2,24]{1,0:T(2,128)S(1)}, f32[2,24]{1,0:T(2,128)S(1)}, u32[]{:S(2)}, u32[]{:S(2)}) collective-permute-start(f32[2,24]{1,0:T(2,128)S(1)} %psum.15), channel_id=1, source_target_pairs={{0,2},{1,3},{2,4},{3,5},{4,6},{5,7},{6,0},{7,1},{8,10},{9,11},{10,... | collective-permute-start | bytes 584 | tf_op jit(solution)/shard_map/ppermute | solution.py:21
  293.8 4.7 %collective-permute-start.32 = (f32[2,24]{1,0:T(2,128)S(1)}, f32[2,24]{1,0:T(2,128)S(1)}, u32[]{:S(2)}, u32[]{:S(2)}) collective-permute-start(f32[2,24]{1,0:T(2,128)S(1)} %psum.15), channel_id=1, source_target_pairs={{0,4},{1,5},{2,6},{3,7},{4,0},{5,1},{6,2},{7,3},{8,12},{9,13},{10,... | collective-permute-start | bytes 584 | tf_op jit(solution)/shard_map/ppermute | solution.py:21
  300.0 2.4 collective-permute-start.30
  303.9 2.1 collective-permute-done.29
  306.2 3.5 %fusion.27 = f32[8192,128]{1,0:T(8,128)S(1)} fusion(bf16[2,192,8192]{2,1,0:T(8,128)(2,1)} %all-gather.2.cloned.1.call-done, f32[192]{0:T(256)S(1)} %squeeze.102, bf16[192,4096]{1,0:T(8,128)(2,1)} %bitcast.160), kind=kOutput, calls=%fused_computation.24 | convolution fusion | flops 407371776 | bytes 7389952 | tf_op jit(solution)/shard_map/dot_general | solution.py:123
  310.0 5.3 %fusion.9 = f32[8192,128]{1,0:T(8,128)} fusion(f32[8192,128]{1,0:T(8,128)S(1)} %fusion.27, bf16[2,192,8192]{2,1,0:T(8,128)(2,1)S(1)} %copy-done.7, f32[192]{0:T(256)S(1)} %div.129, bf16[8192,4096]{1,0:T(8,128)(2,1)} %param.5, bf16[192,4096]{1,0:T(8,128)(2,1)} %bitcast.163), kind=kOutput, calls=%fused_computation.10 | convolution fusion | flops 411566080 | bytes 13681664 | tf_op jit(solution)/shard_map/dot_general | solution.py:123
  (127 shorter events, 38.1 us)
Async XLA Ops:
  7.2 299.0 %all-gather.2.cloned.1.call-start = ((), (), s32[]{:S(2)}) async-start(), calls=%async_computation | async-start | bytes 7077888 | tf_op jit(solution)/shard_map/all_gather | solution.py:90
  9.8 12.1 %collective-permute-start = (bf16[48,4096]{1,0:T(8,128)(2,1)S(1)}, bf16[48,4096]{1,0:T(8,128)(2,1)S(1)}, u32[]{:S(2)}, u32[]{:S(2)}) collective-permute-start(bf16[48,4096]{1,0:T(8,128)(2,1)S(1)} %fusion.24), channel_id=1, source_target_pairs={{0,16},{8,24},{16,0},{24,8},{1,17},{9,25},{17,1},{25,9},{2,18},{10... | collective-permute-start | bytes 1179656 | tf_op jit(solution)/shard_map/ppermute | solution.py:33
  46.4 19.8 %collective-permute-start.2 = (f16[4,24,4096]{2,1,0:T(8,128)(2,1)}, f16[4,24,4096]{2,1,0:T(8,128)(2,1)S(1)}, u32[]{:S(2)}, u32[]{:S(2)}) collective-permute-start(f16[4,24,4096]{2,1,0:T(8,128)(2,1)} %fusion.29), channel_id=1, source_target_pairs={{0,1},{1,0},{2,3},{3,2},{4,5},{5,4},{6,7},{7,6},{8,9},{9,8},{10,11... | collective-permute-start | bytes 2359304 | tf_op jit(solution)/shard_map/ppermute | solution.py:50
  64.5 35.6 %collective-permute-start.6 = (f16[4,24,4096]{2,1,0:T(8,128)(2,1)S(1)}, f16[4,24,4096]{2,1,0:T(8,128)(2,1)S(1)}, u32[]{:S(2)}, u32[]{:S(2)}) collective-permute-start(f16[4,24,4096]{2,1,0:T(8,128)(2,1)S(1)} %fusion.30), channel_id=1, source_target_pairs={{0,1},{1,0},{2,3},{3,2},{4,5},{5,4},{6,7},{7,6},{8,9},{9,8},{10,11... | collective-permute-start | bytes 2359304 | tf_op jit(solution)/shard_map/ppermute | solution.py:50
  68.4 36.5 %collective-permute-start.3 = (f16[24,4096]{1,0:T(8,128)(2,1)S(1)}, f16[24,4096]{1,0:T(8,128)(2,1)S(1)}, u32[]{:S(2)}, u32[]{:S(2)}) collective-permute-start(f16[24,4096]{1,0:T(8,128)(2,1)S(1)} %get-tuple-element.36), channel_id=1, source_target_pairs={{0,2},{1,3},{2,4},{3,5},{4,6},{5,7},{6,0},{7,1},{8,10},{9,11},{10,... | collective-permute-start | bytes 589832 | tf_op jit(solution)/shard_map/ppermute | solution.py:57
  70.3 36.0 %collective-permute-start.4 = (f16[24,4096]{1,0:T(8,128)(2,1)S(1)}, f16[24,4096]{1,0:T(8,128)(2,1)S(1)}, u32[]{:S(2)}, u32[]{:S(2)}) collective-permute-start(f16[24,4096]{1,0:T(8,128)(2,1)S(1)} %get-tuple-element.38), channel_id=1, source_target_pairs={{0,4},{1,5},{2,6},{3,7},{4,0},{5,1},{6,2},{7,3},{8,12},{9,13},{10,... | collective-permute-start | bytes 589832 | tf_op jit(solution)/shard_map/ppermute | solution.py:57
  72.8 33.5 %collective-permute-start.5 = (f16[24,4096]{1,0:T(8,128)(2,1)S(1)}, f16[24,4096]{1,0:T(8,128)(2,1)S(1)}, u32[]{:S(2)}, u32[]{:S(2)}) collective-permute-start(f16[24,4096]{1,0:T(8,128)(2,1)S(1)} %get-tuple-element.37), channel_id=1, source_target_pairs={{0,6},{1,7},{2,0},{3,1},{4,2},{5,3},{6,4},{7,5},{8,14},{9,15},{10,... | collective-permute-start | bytes 589832 | tf_op jit(solution)/shard_map/ppermute | solution.py:57
  100.5 13.8 %collective-permute-start.7 = (f16[24,4096]{1,0:T(8,128)(2,1)S(1)}, f16[24,4096]{1,0:T(8,128)(2,1)S(1)}, u32[]{:S(2)}, u32[]{:S(2)}) collective-permute-start(f16[24,4096]{1,0:T(8,128)(2,1)S(1)} %get-tuple-element.39), channel_id=1, source_target_pairs={{0,2},{1,3},{2,4},{3,5},{4,6},{5,7},{6,0},{7,1},{8,10},{9,11},{10,... | collective-permute-start | bytes 589832 | tf_op jit(solution)/shard_map/ppermute | solution.py:57
  102.2 30.3 %collective-permute-start.8 = (f16[24,4096]{1,0:T(8,128)(2,1)S(1)}, f16[24,4096]{1,0:T(8,128)(2,1)S(1)}, u32[]{:S(2)}, u32[]{:S(2)}) collective-permute-start(f16[24,4096]{1,0:T(8,128)(2,1)S(1)} %get-tuple-element.41), channel_id=1, source_target_pairs={{0,4},{1,5},{2,6},{3,7},{4,0},{5,1},{6,2},{7,3},{8,12},{9,13},{10,... | collective-permute-start | bytes 589832 | tf_op jit(solution)/shard_map/ppermute | solution.py:57
  104.9 27.6 %collective-permute-start.9 = (f16[24,4096]{1,0:T(8,128)(2,1)S(1)}, f16[24,4096]{1,0:T(8,128)(2,1)S(1)}, u32[]{:S(2)}, u32[]{:S(2)}) collective-permute-start(f16[24,4096]{1,0:T(8,128)(2,1)S(1)} %get-tuple-element.40), channel_id=1, source_target_pairs={{0,6},{1,7},{2,0},{3,1},{4,2},{5,3},{6,4},{7,5},{8,14},{9,15},{10,... | collective-permute-start | bytes 589832 | tf_op jit(solution)/shard_map/ppermute | solution.py:57
  139.2 23.9 %collective-permute-start.10 = (f32[24,4096]{1,0:T(8,128)S(1)}, f32[24,4096]{1,0:T(8,128)S(1)}, u32[]{:S(2)}, u32[]{:S(2)}) collective-permute-start(f32[24,4096]{1,0:T(8,128)S(1)} %get-tuple-element.35), channel_id=1, source_target_pairs={{0,0},{1,1},{2,8},{3,9},{4,16},{5,17},{6,24},{7,25},{8,2},{9,3},{1... | collective-permute-start | bytes 1179656 | tf_op jit(solution)/shard_map/ppermute | solution.py:116
  139.9 39.3 %collective-permute-start.11 = (f32[24,4096]{1,0:T(8,128)S(1)}, f32[24,4096]{1,0:T(8,128)S(1)}, u32[]{:S(2)}, u32[]{:S(2)}) collective-permute-start(f32[24,4096]{1,0:T(8,128)S(1)} %get-tuple-element.34), channel_id=1, source_target_pairs={{0,1},{1,0},{2,9},{3,8},{4,17},{5,16},{6,25},{7,24},{8,3},{9,2},{1... | collective-permute-start | bytes 1179656 | tf_op jit(solution)/shard_map/ppermute | solution.py:116
  141.8 55.4 %collective-permute-start.14 = (f32[2,24]{1,0:T(2,128)S(1)}, f32[2,24]{1,0:T(2,128)S(1)}, u32[]{:S(2)}, u32[]{:S(2)}) collective-permute-start(f32[2,24]{1,0:T(2,128)S(1)} %psum.14), channel_id=1, source_target_pairs={{0,7},{1,0},{2,1},{3,2},{4,3},{5,4},{6,5},{7,6},{8,15},{9,8},{10,9... | collective-permute-start | bytes 584 | tf_op jit(solution)/shard_map/ppermute | solution.py:21
  162.9 41.2 %collective-permute-start.15 = (f32[2,24]{1,0:T(2,128)S(1)}, f32[2,24]{1,0:T(2,128)S(1)}, u32[]{:S(2)}, u32[]{:S(2)}) collective-permute-start(f32[2,24]{1,0:T(2,128)S(1)} %psum.14), channel_id=1, source_target_pairs={{0,6},{1,7},{2,0},{3,1},{4,2},{5,3},{6,4},{7,5},{8,14},{9,15},{10,... | collective-permute-start | bytes 584 | tf_op jit(solution)/shard_map/ppermute | solution.py:21
  163.1 41.0 %collective-permute-start.16 = (f32[2,24]{1,0:T(2,128)S(1)}, f32[2,24]{1,0:T(2,128)S(1)}, u32[]{:S(2)}, u32[]{:S(2)}) collective-permute-start(f32[2,24]{1,0:T(2,128)S(1)} %psum.14), channel_id=1, source_target_pairs={{0,5},{1,6},{2,7},{3,0},{4,1},{5,2},{6,3},{7,4},{8,13},{9,14},{10,... | collective-permute-start | bytes 584 | tf_op jit(solution)/shard_map/ppermute | solution.py:21
  163.1 42.4 %collective-permute-start.17 = (f32[2,24]{1,0:T(2,128)S(1)}, f32[2,24]{1,0:T(2,128)S(1)}, u32[]{:S(2)}, u32[]{:S(2)}) collective-permute-start(f32[2,24]{1,0:T(2,128)S(1)} %psum.14), channel_id=1, source_target_pairs={{0,4},{1,5},{2,6},{3,7},{4,0},{5,1},{6,2},{7,3},{8,12},{9,13},{10,... | collective-permute-start | bytes 584 | tf_op jit(solution)/shard_map/ppermute | solution.py:21
  179.7 16.8 %collective-permute-start.12 = (bf16[48,4096]{1,0:T(8,128)(2,1)S(1)}, bf16[48,4096]{1,0:T(8,128)(2,1)S(1)}, u32[]{:S(2)}, u32[]{:S(2)}) collective-permute-start(bf16[48,4096]{1,0:T(8,128)(2,1)S(1)} %fusion.46), channel_id=1, source_target_pairs={{0,16},{8,24},{16,0},{24,8},{1,17},{9,25},{17,1},{25,9},{2,18},{10... | collective-permute-start | bytes 1179656 | tf_op jit(solution)/shard_map/ppermute | solution.py:33
  197.1 13.7 %collective-permute-start.13 = (bf16[2,48,4096]{2,1,0:T(8,128)(2,1)S(1)}, bf16[2,48,4096]{2,1,0:T(8,128)(2,1)S(1)}, u32[]{:S(2)}, u32[]{:S(2)}) collective-permute-start(bf16[2,48,4096]{2,1,0:T(8,128)(2,1)S(1)} %fusion.35), channel_id=1, source_target_pairs={{0,8},{8,0},{16,24},{24,16},{1,9},{9,1},{17,25},{25,17},{2,10},{10... | collective-permute-start | bytes 2359304 | tf_op jit(solution)/shard_map/ppermute | solution.py:35
  197.2 8.3 %collective-permute-start.18 = (f32[2,24]{1,0:T(2,128)S(1)}, f32[2,24]{1,0:T(2,128)S(1)}, u32[]{:S(2)}, u32[]{:S(2)}) collective-permute-start(f32[2,24]{1,0:T(2,128)S(1)} %psum.14), channel_id=1, source_target_pairs={{0,3},{1,4},{2,5},{3,6},{4,7},{5,0},{6,1},{7,2},{8,11},{9,12},{10,... | collective-permute-start | bytes 584 | tf_op jit(solution)/shard_map/ppermute | solution.py:21
  204.1 6.3 %collective-permute-start.20 = (f32[2,24]{1,0:T(2,128)S(1)}, f32[2,24]{1,0:T(2,128)S(1)}, u32[]{:S(2)}, u32[]{:S(2)}) collective-permute-start(f32[2,24]{1,0:T(2,128)S(1)} %psum.14), channel_id=1, source_target_pairs={{0,1},{1,2},{2,3},{3,4},{4,5},{5,6},{6,7},{7,0},{8,9},{9,10},{10,1... | collective-permute-start | bytes 584 | tf_op jit(solution)/shard_map/ppermute | solution.py:21
  229.7 19.0 %collective-permute-start.21 = (f16[4,24,4096]{2,1,0:T(8,128)(2,1)}, f16[4,24,4096]{2,1,0:T(8,128)(2,1)}, u32[]{:S(2)}, u32[]{:S(2)}) collective-permute-start(f16[4,24,4096]{2,1,0:T(8,128)(2,1)} %fusion.31), channel_id=1, source_target_pairs={{0,1},{1,0},{2,3},{3,2},{4,5},{5,4},{6,7},{7,6},{8,9},{9,8},{10,11... | collective-permute-start | bytes 2359304 | tf_op jit(solution)/shard_map/ppermute | solution.py:50
  246.5 18.8 %collective-permute-start.25 = (f16[4,24,4096]{2,1,0:T(8,128)(2,1)S(1)}, f16[4,24,4096]{2,1,0:T(8,128)(2,1)S(1)}, u32[]{:S(2)}, u32[]{:S(2)}) collective-permute-start(f16[4,24,4096]{2,1,0:T(8,128)(2,1)S(1)} %fusion.32), channel_id=1, source_target_pairs={{0,1},{1,0},{2,3},{3,2},{4,5},{5,4},{6,7},{7,6},{8,9},{9,8},{10,11... | collective-permute-start | bytes 2359304 | tf_op jit(solution)/shard_map/ppermute | solution.py:50
  250.3 17.7 %collective-permute-start.22 = (f16[24,4096]{1,0:T(8,128)(2,1)S(1)}, f16[24,4096]{1,0:T(8,128)(2,1)S(1)}, u32[]{:S(2)}, u32[]{:S(2)}) collective-permute-start(f16[24,4096]{1,0:T(8,128)(2,1)S(1)} %get-tuple-element.28), channel_id=1, source_target_pairs={{0,2},{1,3},{2,4},{3,5},{4,6},{5,7},{6,0},{7,1},{8,10},{9,11},{10,... | collective-permute-start | bytes 589832 | tf_op jit(solution)/shard_map/ppermute | solution.py:57
  250.4 19.2 %collective-permute-start.23 = (f16[24,4096]{1,0:T(8,128)(2,1)S(1)}, f16[24,4096]{1,0:T(8,128)(2,1)S(1)}, u32[]{:S(2)}, u32[]{:S(2)}) collective-permute-start(f16[24,4096]{1,0:T(8,128)(2,1)S(1)} %get-tuple-element.30), channel_id=1, source_target_pairs={{0,4},{1,5},{2,6},{3,7},{4,0},{5,1},{6,2},{7,3},{8,12},{9,13},{10,... | collective-permute-start | bytes 589832 | tf_op jit(solution)/shard_map/ppermute | solution.py:57
  252.7 16.9 %collective-permute-start.24 = (f16[24,4096]{1,0:T(8,128)(2,1)S(1)}, f16[24,4096]{1,0:T(8,128)(2,1)S(1)}, u32[]{:S(2)}, u32[]{:S(2)}) collective-permute-start(f16[24,4096]{1,0:T(8,128)(2,1)S(1)} %get-tuple-element.29), channel_id=1, source_target_pairs={{0,6},{1,7},{2,0},{3,1},{4,2},{5,3},{6,4},{7,5},{8,14},{9,15},{10,... | collective-permute-start | bytes 589832 | tf_op jit(solution)/shard_map/ppermute | solution.py:57
  265.7 9.7 %collective-permute-start.26 = (f16[24,4096]{1,0:T(8,128)(2,1)S(1)}, f16[24,4096]{1,0:T(8,128)(2,1)S(1)}, u32[]{:S(2)}, u32[]{:S(2)}) collective-permute-start(f16[24,4096]{1,0:T(8,128)(2,1)S(1)} %get-tuple-element.31), channel_id=1, source_target_pairs={{0,2},{1,3},{2,4},{3,5},{4,6},{5,7},{6,0},{7,1},{8,10},{9,11},{10,... | collective-permute-start | bytes 589832 | tf_op jit(solution)/shard_map/ppermute | solution.py:57
  265.8 17.0 %collective-permute-start.27 = (f16[24,4096]{1,0:T(8,128)(2,1)S(1)}, f16[24,4096]{1,0:T(8,128)(2,1)S(1)}, u32[]{:S(2)}, u32[]{:S(2)}) collective-permute-start(f16[24,4096]{1,0:T(8,128)(2,1)S(1)} %get-tuple-element.33), channel_id=1, source_target_pairs={{0,4},{1,5},{2,6},{3,7},{4,0},{5,1},{6,2},{7,3},{8,12},{9,13},{10,... | collective-permute-start | bytes 589832 | tf_op jit(solution)/shard_map/ppermute | solution.py:57
  268.0 14.8 %collective-permute-start.28 = (f16[24,4096]{1,0:T(8,128)(2,1)S(1)}, f16[24,4096]{1,0:T(8,128)(2,1)S(1)}, u32[]{:S(2)}, u32[]{:S(2)}) collective-permute-start(f16[24,4096]{1,0:T(8,128)(2,1)S(1)} %get-tuple-element.32), channel_id=1, source_target_pairs={{0,6},{1,7},{2,0},{3,1},{4,2},{5,3},{6,4},{7,5},{8,14},{9,15},{10,... | collective-permute-start | bytes 589832 | tf_op jit(solution)/shard_map/ppermute | solution.py:57
  289.0 16.9 %collective-permute-start.35 = (f32[2,24]{1,0:T(2,128)S(1)}, f32[2,24]{1,0:T(2,128)S(1)}, u32[]{:S(2)}, u32[]{:S(2)}) collective-permute-start(f32[2,24]{1,0:T(2,128)S(1)} %psum.15), channel_id=1, source_target_pairs={{0,1},{1,2},{2,3},{3,4},{4,5},{5,6},{6,7},{7,0},{8,9},{9,10},{10,1... | collective-permute-start | bytes 584 | tf_op jit(solution)/shard_map/ppermute | solution.py:21
  289.0 10.9 %collective-permute-start.34 = (f32[2,24]{1,0:T(2,128)S(1)}, f32[2,24]{1,0:T(2,128)S(1)}, u32[]{:S(2)}, u32[]{:S(2)}) collective-permute-start(f32[2,24]{1,0:T(2,128)S(1)} %psum.15), channel_id=1, source_target_pairs={{0,2},{1,3},{2,4},{3,5},{4,6},{5,7},{6,0},{7,1},{8,10},{9,11},{10,... | collective-permute-start | bytes 584 | tf_op jit(solution)/shard_map/ppermute | solution.py:21
  293.8 8.5 %collective-permute-start.33 = (f32[2,24]{1,0:T(2,128)S(1)}, f32[2,24]{1,0:T(2,128)S(1)}, u32[]{:S(2)}, u32[]{:S(2)}) collective-permute-start(f32[2,24]{1,0:T(2,128)S(1)} %psum.15), channel_id=1, source_target_pairs={{0,3},{1,4},{2,5},{3,6},{4,7},{5,0},{6,1},{7,2},{8,11},{9,12},{10,... | collective-permute-start | bytes 584 | tf_op jit(solution)/shard_map/ppermute | solution.py:21
  293.8 10.0 %collective-permute-start.32 = (f32[2,24]{1,0:T(2,128)S(1)}, f32[2,24]{1,0:T(2,128)S(1)}, u32[]{:S(2)}, u32[]{:S(2)}) collective-permute-start(f32[2,24]{1,0:T(2,128)S(1)} %psum.15), channel_id=1, source_target_pairs={{0,4},{1,5},{2,6},{3,7},{4,0},{5,1},{6,2},{7,3},{8,12},{9,13},{10,... | collective-permute-start | bytes 584 | tf_op jit(solution)/shard_map/ppermute | solution.py:21
  (13 other events, 135.3 us)
Sparse Core Ops, SparseCore 0:
  22.7 131.6 all-gather.1

commit v3 on v2

--- a/solution.py
+++ b/solution.py
@@ -16,14 +16,13 @@
 
 
 def gather_small(value, col_count, col_index):
-    arrived = [value]
-    for k in range(1, col_count):
-        arrived.append(lax.ppermute(value, "col", [(c, (c + k) % col_count) for c in range(col_count)]))
-    place = lax.broadcasted_iota(jnp.int32, (col_count,) + value.shape, 0)
-    out = jnp.zeros(place.shape, value.dtype)
-    for k, got in enumerate(arrived):
-        out = jnp.where(place == (col_index - k + col_count) % col_count, got[None], out)
-    return out
+    block = value[None]
+    while block.shape[0] < col_count:
+        step = block.shape[0]
+        got = lax.ppermute(block, "col", [(c, c ^ step) for c in range(col_count)])
+        first = col_index // step % 2 == 0
+        block = jnp.where(first, jnp.concatenate([block, got]), jnp.concatenate([got, block]))
+    return block
 
 
 def gather_rows(value, row_count, row_index):
@@ -101,8 +100,6 @@
         mine = jnp.concatenate(pieces, axis=1) / scale_mine
         norm = jnp.sum(forward[step].astype(jnp.float32) * mine, axis=1)
         sums = lax.psum(jnp.stack([norm, jnp.sum(mine, axis=1)]), "row")
-        sums_all = gather_small(sums, col_count, col_index)
-        normals[step] = sums_all[:, 0].reshape(seq_total)
         outputs[step] = mine / sums[0][:, None]
         if step == 1:
             halves = outputs[step].reshape(local_seqs, ratio, block_dst)
@@ -115,8 +112,12 @@
                         moves.append((r * col_count + c, (c // ratio) * col_count + r * ratio + (c + p) % ratio))
                 arrived.append(lax.ppermute(part, ("row", "col"), moves))
             beta = in_order(arrived, col_index % ratio).reshape(row_seqs, block_dst)
+            beta, sums = lax.optimization_barrier((beta, sums))
+            sums_all = gather_small(sums, col_count, col_index)
+            normals[step] = sums_all[:, 0].reshape(seq_total)
             scale = (16777216.0 * sums_all[:, 0] / sums_all[:, 1]).reshape(seq_total, 1)
             scale_mine = (16777216.0 * sums[0] / sums[1])[:, None]
+    normals[0] = gather_small(sums, col_count, col_index)[:, 0].reshape(seq_total)
     totals = jnp.zeros((block_src, DW), jnp.float32)
     for step in (1, 0):
         scaled = (forward_all[step].astype(jnp.float32) / normals[step][:, None]).astype(jnp.bfloat16)

time: 323 us -> 359 us (1.11)
  waiting for transfers between devices: 101 us -> 162 us
  starting transfers between devices: 99.3 us -> 67.7 us
  other arithmetic: 14.3 us -> 18.3 us
    ppermute x14 -> x6, starting transfers between devices: 59.1 us -> 5.5 us  [gather_small(): got = lax.ppermute(block, 'col', [(c, c ^ step) for c in range(col_count)])]
    ppermute x4, waiting for transfers between devices: 38.7 us -> 77.3 us  [reduce_scatter(): got = lax.ppermute(away, 'col', [(c, c ^ 1) for c in range(col_count)])]
    ppermute x2, starting transfers between devices: 14.1 us -> 32.5 us  [gather_rows(): lax.ppermute(value, 'row', [(r, (r + 2 * k) % row_count) for r in range(r...]
    ppermute x14 -> x6, waiting for transfers between devices: 7 us -> 17 us  [gather_small(): got = lax.ppermute(block, 'col', [(c, c ^ step) for c in range(col_count)])]
    ppermute x2, waiting for transfers between devices: 0.01 us -> 6.87 us  [on_device(): arrived.append(lax.ppermute(part, ('row', 'col'), moves))]
    ppermute x12, waiting for transfers between devices: 39.3 us -> 43.6 us  [reduce_scatter(): lax.ppermute(piece, 'col', [(c, (c + 2 * k) % col_count) for c in range(c...]
  transfers between devices with their start and end apart: 37 -> 29, of which waited for: 14 -> 20; matrix products, arithmetic and copies ran while one was open for 26% -> 13% of each run, Pallas kernels for 0% -> 0%
where the time goes in v3:
time: 359 us; the launch traced here: 358 us
  waiting for transfers between devices  162 us (45%)
  matrix products  79.8 us (22%)
  starting transfers between devices  67.7 us (19%)
  other arithmetic  18.3 us (5%)
  between operations  14.4 us (4%)
  blocking collectives  11.8 us (3%)
  local copies, waits for them, and re-layouts  4.3 us (1%)
    ppermute x4, waiting for transfers between devices, reduce_scatter(): got = lax.ppermute(away, 'col', [(c, c ^ 1) for c in range(col_count)])  77.3 us
    dot_general x4, matrix products, on_device(): lax.dot_general(weighted_back, transition[rows], (((1,), (1,)), ((), ()))...  69.2 us
    ppermute x12, waiting for transfers between devices, reduce_scatter(): lax.ppermute(piece, 'col', [(c, (c + 2 * k) % col_count) for c in range(c...  43.6 us
    ppermute x2, starting transfers between devices, gather_rows(): lax.ppermute(value, 'row', [(r, (r + 2 * k) % row_count) for r in range(r...  32.5 us
    ppermute x12, starting transfers between devices, reduce_scatter(): lax.ppermute(piece, 'col', [(c, (c + 2 * k) % col_count) for c in range(c...  19.3 us
    ppermute x6, waiting for transfers between devices, gather_small(): got = lax.ppermute(block, 'col', [(c, c ^ step) for c in range(col_count)])  17 us
    ppermute x2, waiting for transfers between devices, gather_rows(): lax.ppermute(value, 'row', [(r, (r + 2 * k) % row_count) for r in range(r...  14.9 us
    psum x2, blocking collectives, on_device(): sums = lax.psum(jnp.stack([norm, jnp.sum(mine, axis=1)]), 'row')  11.8 us
  transfers between devices with their start and end apart: 29, of which 20 were waited for; matrix products, arithmetic and copies ran while one was open for 13% of the time, Pallas kernels for 0%

profile of v3, /device:TPU:0, one launch (start us, length us, event | category | flops | bytes accessed | tf_op | source)
XLA Modules:
  0.0 358.3 jit_solution(12738687303159449353)
XLA Ops:
  9.8 3.0 collective-permute-start
  12.8 9.1 %collective-permute-done = bf16[48,4096]{1,0:T(8,128)(2,1)S(1)} collective-permute-done((bf16[48,4096]{1,0:T(8,128)(2,1)S(1)}, bf16[48,4096]{1,0:T(8,128)(2,1)S(1)}, u32[]{:S(2)}, u32[]{:S(2)}) %collective-permute-start) | collective-permute-done | bytes 393248 | tf_op jit(solution)/shard_map/ppermute | solution.py:32
  22.6 2.4 collective-permute-done.1
  27.0 16.5 %fusion.12 = f32[192,4096]{1,0:T(8,128)S(1)} fusion(bf16[192,4096]{1,0:T(8,128)(2,1)S(1)} %bitcast.158, bf16[8192,4096]{1,0:T(8,128)(2,1)} %param.5), kind=kOutput, calls=%fused_computation.15 | convolution fusion | flops 6443237376 | bytes 38273024 | tf_op jit(solution)/shard_map/dot_general | solution.py:93
  44.6 17.8 %fusion.18 = f32[192,4096]{1,0:T(8,128)} fusion(bf16[192,4096]{1,0:T(8,128)(2,1)S(1)} %bitcast.159, bf16[8192,4096]{1,0:T(8,128)(2,1)} %param.5), kind=kOutput, calls=%fused_computation.17 | convolution fusion | flops 6443237376 | bytes 38273024 | tf_op jit(solution)/shard_map/dot_general | solution.py:93
  65.9 18.5 %collective-permute-done.6 = f16[4,24,4096]{2,1,0:T(8,128)(2,1)} collective-permute-done((f16[4,24,4096]{2,1,0:T(8,128)(2,1)S(1)}, f16[4,24,4096]{2,1,0:T(8,128)(2,1)}, u32[]{:S(2)}, u32[]{:S(2)}) %collective-permute-start.6) | collective-permute-done | bytes 786464 | tf_op jit(solution)/shard_map/ppermute | solution.py:49
  86.6 3.9 %collective-permute-start.9 = (f16[24,4096]{1,0:T(8,128)(2,1)S(1)}, f16[24,4096]{1,0:T(8,128)(2,1)S(1)}, u32[]{:S(2)}, u32[]{:S(2)}) collective-permute-start(f16[24,4096]{1,0:T(8,128)(2,1)S(1)} %get-tuple-element.44), channel_id=1, source_target_pairs={{0,6},{1,7},{2,0},{3,1},{4,2},{5,3},{6,4},{7,5},{8,14},{9,15},{10,... | collective-permute-start | bytes 589832 | tf_op jit(solution)/shard_map/ppermute | solution.py:56
  91.5 8.9 %collective-permute-done.2 = f16[4,24,4096]{2,1,0:T(8,128)(2,1)S(1)} collective-permute-done((f16[4,24,4096]{2,1,0:T(8,128)(2,1)}, f16[4,24,4096]{2,1,0:T(8,128)(2,1)S(1)}, u32[]{:S(2)}, u32[]{:S(2)}) %collective-permute-start.2) | collective-permute-done | bytes 786464 | tf_op jit(solution)/shard_map/ppermute | solution.py:49
  100.7 3.9 %collective-permute-start.5 = (f16[24,4096]{1,0:T(8,128)(2,1)S(1)}, f16[24,4096]{1,0:T(8,128)(2,1)S(1)}, u32[]{:S(2)}, u32[]{:S(2)}) collective-permute-start(f16[24,4096]{1,0:T(8,128)(2,1)S(1)} %get-tuple-element.41), channel_id=1, source_target_pairs={{0,6},{1,7},{2,0},{3,1},{4,2},{5,3},{6,4},{7,5},{8,14},{9,15},{10,... | collective-permute-start | bytes 589832 | tf_op jit(solution)/shard_map/ppermute | solution.py:56
  105.6 2.2 collective-permute-done.8
  110.1 13.0 %collective-permute-done.4 = f16[24,4096]{1,0:T(8,128)(2,1)S(1)} collective-permute-done((f16[24,4096]{1,0:T(8,128)(2,1)S(1)}, f16[24,4096]{1,0:T(8,128)(2,1)S(1)}, u32[]{:S(2)}, u32[]{:S(2)}) %collective-permute-start.4) | collective-permute-done | bytes 196640 | tf_op jit(solution)/shard_map/ppermute | solution.py:56
  123.5 5.7 %psum.14 = f32[2,24]{1,0:T(2,128)S(1)} all-reduce(f32[2,24]{1,0:T(2,128)S(1)} %pad_maximum_fusion.5), channel_id=1, replica_groups=mesh['row'=4,'col'=8] {'row'}, use_global_device_ids=true, to_apply=%region_2.3 | all-reduce | flops 48 | bytes 384 | tf_op jit(solution)/shard_map/psum | solution.py:102
  130.1 4.5 %collective-permute-start.10 = (f32[24,4096]{1,0:T(8,128)}, f32[24,4096]{1,0:T(8,128)}, u32[]{:S(2)}, u32[]{:S(2)}) collective-permute-start(f32[24,4096]{1,0:T(8,128)} %get-tuple-element.39), channel_id=1, source_target_pairs={{0,0},{1,1},{2,8},{3,9},{4,16},{5,17},{6,24},{7,25},{8,2},{9,3},{1... | collective-permute-start | bytes 1179656 | tf_op jit(solution)/shard_map/ppermute | solution.py:113
  136.2 6.9 %collective-permute-done.11 = f32[24,4096]{1,0:T(8,128)} collective-permute-done((f32[24,4096]{1,0:T(8,128)S(1)}, f32[24,4096]{1,0:T(8,128)}, u32[]{:S(2)}, u32[]{:S(2)}) %collective-permute-start.11) | collective-permute-done | bytes 393248 | tf_op jit(solution)/shard_map/ppermute | solution.py:113
  144.9 29.5 %collective-permute-start.12 = (bf16[48,4096]{1,0:T(8,128)(2,1)S(1)}, bf16[48,4096]{1,0:T(8,128)(2,1)S(1)}, u32[]{:S(2)}, u32[]{:S(2)}) collective-permute-start(bf16[48,4096]{1,0:T(8,128)(2,1)S(1)} %fusion.24), channel_id=1, source_target_pairs={{0,16},{8,24},{16,0},{24,8},{1,17},{9,25},{17,1},{25,9},{2,18},{10... | collective-permute-start | bytes 1179656 | tf_op jit(solution)/shard_map/ppermute | solution.py:32
  174.4 5.8 %collective-permute-done.12 = bf16[48,4096]{1,0:T(8,128)(2,1)S(1)} collective-permute-done((bf16[48,4096]{1,0:T(8,128)(2,1)S(1)}, bf16[48,4096]{1,0:T(8,128)(2,1)S(1)}, u32[]{:S(2)}, u32[]{:S(2)}) %collective-permute-start.12) | collective-permute-done | bytes 393248 | tf_op jit(solution)/shard_map/ppermute | solution.py:32
  182.1 3.2 collective-permute-done.14
  185.5 3.3 collective-permute-done.15
  188.8 3.2 collective-permute-start.16
  197.4 17.0 %fusion.15 = f32[192,4096]{1,0:T(8,128)S(1)} fusion(bf16[192,4096]{1,0:T(8,128)(2,1)} %bitcast.161, bf16[8192,4096]{1,0:T(8,128)(2,1)} %param.5, f32[192]{0:T(256)S(1)} %multiply_divide_fusion), kind=kOutput, calls=%fused_computation.16 | convolution fusion | flops 6443237376 | bytes 38273792 | tf_op jit(solution)/shard_map/dot_general | solution.py:93
  215.4 17.9 %fusion.21 = f32[192,4096]{1,0:T(8,128)} fusion(bf16[192,4096]{1,0:T(8,128)(2,1)} %bitcast.162, bf16[8192,4096]{1,0:T(8,128)(2,1)} %param.5, f32[192]{0:T(256)S(1)} %multiply_divide_fusion), kind=kOutput, calls=%fused_computation.18 | convolution fusion | flops 6443237376 | bytes 38273792 | tf_op jit(solution)/shard_map/dot_general | solution.py:93
  237.2 35.0 %collective-permute-done.21 = f16[4,24,4096]{2,1,0:T(8,128)(2,1)S(1)} collective-permute-done((f16[4,24,4096]{2,1,0:T(8,128)(2,1)S(1)}, f16[4,24,4096]{2,1,0:T(8,128)(2,1)S(1)}, u32[]{:S(2)}, u32[]{:S(2)}) %collective-permute-start.21) | collective-permute-done | bytes 786464 | tf_op jit(solution)/shard_map/ppermute | solution.py:49
  272.6 2.8 collective-permute-start.24
  277.7 15.0 %collective-permute-done.17 = f16[4,24,4096]{2,1,0:T(8,128)(2,1)S(1)} collective-permute-done((f16[4,24,4096]{2,1,0:T(8,128)(2,1)S(1)}, f16[4,24,4096]{2,1,0:T(8,128)(2,1)S(1)}, u32[]{:S(2)}, u32[]{:S(2)}) %collective-permute-start.17) | collective-permute-done | bytes 786464 | tf_op jit(solution)/shard_map/ppermute | solution.py:49
  293.1 3.4 collective-permute-start.20
  297.6 8.2 %collective-permute-done.23 = f16[24,4096]{1,0:T(8,128)(2,1)S(1)} collective-permute-done((f16[24,4096]{1,0:T(8,128)(2,1)S(1)}, f16[24,4096]{1,0:T(8,128)(2,1)S(1)}, u32[]{:S(2)}, u32[]{:S(2)}) %collective-permute-start.23) | collective-permute-done | bytes 196640 | tf_op jit(solution)/shard_map/ppermute | solution.py:56
  307.8 16.1 %collective-permute-done.19 = f16[24,4096]{1,0:T(8,128)(2,1)S(1)} collective-permute-done((f16[24,4096]{1,0:T(8,128)(2,1)S(1)}, f16[24,4096]{1,0:T(8,128)(2,1)S(1)}, u32[]{:S(2)}, u32[]{:S(2)}) %collective-permute-start.19) | collective-permute-done | bytes 196640 | tf_op jit(solution)/shard_map/ppermute | solution.py:56
  324.4 6.2 %psum.15 = f32[2,24]{1,0:T(2,128)S(1)} all-reduce(f32[2,24]{1,0:T(2,128)S(1)} %pad_maximum_fusion.6), channel_id=1, replica_groups=mesh['row'=4,'col'=8] {'row'}, use_global_device_ids=true, to_apply=%region_5.6 | all-reduce | flops 48 | bytes 384 | tf_op jit(solution)/shard_map/psum | solution.py:102
  330.8 3.4 collective-permute-done.25
  334.4 3.4 collective-permute-done.26
  342.5 3.5 fusion.28
  346.2 5.3 %fusion.9 = f32[8192,128]{1,0:T(8,128)} fusion(f32[8192,128]{1,0:T(8,128)S(1)} %fusion.28, bf16[2,192,8192]{2,1,0:T(8,128)(2,1)S(1)} %copy-done.9, f32[192]{0:T(256)S(1)} %div.145, bf16[8192,4096]{1,0:T(8,128)(2,1)} %param.5, bf16[192,4096]{1,0:T(8,128)(2,1)} %bitcast.163), kind=kOutput, calls=%fused_computation.10 | convolution fusion | flops 411566080 | bytes 13681664 | tf_op jit(solution)/shard_map/dot_general | solution.py:124
  (108 shorter events, 45.7 us)
Async XLA Ops:
  7.2 335.3 %all-gather.2.cloned.1.call-start = ((), (), s32[]{:S(2)}) async-start(), calls=%async_computation | async-start | bytes 7077888 | tf_op jit(solution)/shard_map/all_gather | solution.py:89
  9.8 12.1 %collective-permute-start = (bf16[48,4096]{1,0:T(8,128)(2,1)S(1)}, bf16[48,4096]{1,0:T(8,128)(2,1)S(1)}, u32[]{:S(2)}, u32[]{:S(2)}) collective-permute-start(bf16[48,4096]{1,0:T(8,128)(2,1)S(1)} %fusion.25), channel_id=1, source_target_pairs={{0,16},{8,24},{16,0},{24,8},{1,17},{9,25},{17,1},{25,9},{2,18},{10... | collective-permute-start | bytes 1179656 | tf_op jit(solution)/shard_map/ppermute | solution.py:32
  22.5 2.5 collective-permute-start.1
  63.9 20.6 %collective-permute-start.6 = (f16[4,24,4096]{2,1,0:T(8,128)(2,1)S(1)}, f16[4,24,4096]{2,1,0:T(8,128)(2,1)}, u32[]{:S(2)}, u32[]{:S(2)}) collective-permute-start(f16[4,24,4096]{2,1,0:T(8,128)(2,1)S(1)} %fusion.31), channel_id=1, source_target_pairs={{0,1},{1,0},{2,3},{3,2},{4,5},{5,4},{6,7},{7,6},{8,9},{9,8},{10,11... | collective-permute-start | bytes 2359304 | tf_op jit(solution)/shard_map/ppermute | solution.py:49
  65.6 34.7 %collective-permute-start.2 = (f16[4,24,4096]{2,1,0:T(8,128)(2,1)}, f16[4,24,4096]{2,1,0:T(8,128)(2,1)S(1)}, u32[]{:S(2)}, u32[]{:S(2)}) collective-permute-start(f16[4,24,4096]{2,1,0:T(8,128)(2,1)} %fusion.30), channel_id=1, source_target_pairs={{0,1},{1,0},{2,3},{3,2},{4,5},{5,4},{6,7},{7,6},{8,9},{9,8},{10,11... | collective-permute-start | bytes 2359304 | tf_op jit(solution)/shard_map/ppermute | solution.py:49
  86.6 18.0 %collective-permute-start.9 = (f16[24,4096]{1,0:T(8,128)(2,1)S(1)}, f16[24,4096]{1,0:T(8,128)(2,1)S(1)}, u32[]{:S(2)}, u32[]{:S(2)}) collective-permute-start(f16[24,4096]{1,0:T(8,128)(2,1)S(1)} %get-tuple-element.44), channel_id=1, source_target_pairs={{0,6},{1,7},{2,0},{3,1},{4,2},{5,3},{6,4},{7,5},{8,14},{9,15},{10,... | collective-permute-start | bytes 589832 | tf_op jit(solution)/shard_map/ppermute | solution.py:56
  90.4 17.4 %collective-permute-start.8 = (f16[24,4096]{1,0:T(8,128)(2,1)S(1)}, f16[24,4096]{1,0:T(8,128)(2,1)S(1)}, u32[]{:S(2)}, u32[]{:S(2)}) collective-permute-start(f16[24,4096]{1,0:T(8,128)(2,1)S(1)} %get-tuple-element.45), channel_id=1, source_target_pairs={{0,4},{1,5},{2,6},{3,7},{4,0},{5,1},{6,2},{7,3},{8,12},{9,13},{10,... | collective-permute-start | bytes 589832 | tf_op jit(solution)/shard_map/ppermute | solution.py:56
  90.4 17.4 %collective-permute-start.7 = (f16[24,4096]{1,0:T(8,128)(2,1)S(1)}, f16[24,4096]{1,0:T(8,128)(2,1)S(1)}, u32[]{:S(2)}, u32[]{:S(2)}) collective-permute-start(f16[24,4096]{1,0:T(8,128)(2,1)S(1)} %get-tuple-element.43), channel_id=1, source_target_pairs={{0,2},{1,3},{2,4},{3,5},{4,6},{5,7},{6,0},{7,1},{8,10},{9,11},{10,... | collective-permute-start | bytes 589832 | tf_op jit(solution)/shard_map/ppermute | solution.py:56
  100.7 22.4 %copy-start.5 = (bf16[2,24,8192]{2,1,0:T(8,128)(2,1)S(1)}, bf16[2,24,8192]{2,1,0:T(8,128)(2,1)}, u32[]{:S(2)}) copy-start(bf16[2,24,8192]{2,1,0:T(8,128)(2,1)} %param.8) | copy-start | bytes 2359300
  100.7 9.3 %collective-permute-start.5 = (f16[24,4096]{1,0:T(8,128)(2,1)S(1)}, f16[24,4096]{1,0:T(8,128)(2,1)S(1)}, u32[]{:S(2)}, u32[]{:S(2)}) collective-permute-start(f16[24,4096]{1,0:T(8,128)(2,1)S(1)} %get-tuple-element.41), channel_id=1, source_target_pairs={{0,6},{1,7},{2,0},{3,1},{4,2},{5,3},{6,4},{7,5},{8,14},{9,15},{10,... | collective-permute-start | bytes 589832 | tf_op jit(solution)/shard_map/ppermute | solution.py:56
  104.6 18.4 %collective-permute-start.4 = (f16[24,4096]{1,0:T(8,128)(2,1)S(1)}, f16[24,4096]{1,0:T(8,128)(2,1)S(1)}, u32[]{:S(2)}, u32[]{:S(2)}) collective-permute-start(f16[24,4096]{1,0:T(8,128)(2,1)S(1)} %get-tuple-element.42), channel_id=1, source_target_pairs={{0,4},{1,5},{2,6},{3,7},{4,0},{5,1},{6,2},{7,3},{8,12},{9,13},{10,... | collective-permute-start | bytes 589832 | tf_op jit(solution)/shard_map/ppermute | solution.py:56
  104.6 18.4 %collective-permute-start.3 = (f16[24,4096]{1,0:T(8,128)(2,1)S(1)}, f16[24,4096]{1,0:T(8,128)(2,1)S(1)}, u32[]{:S(2)}, u32[]{:S(2)}) collective-permute-start(f16[24,4096]{1,0:T(8,128)(2,1)S(1)} %get-tuple-element.40), channel_id=1, source_target_pairs={{0,2},{1,3},{2,4},{3,5},{4,6},{5,7},{6,0},{7,1},{8,10},{9,11},{10,... | collective-permute-start | bytes 589832 | tf_op jit(solution)/shard_map/ppermute | solution.py:56
  130.1 6.1 %collective-permute-start.10 = (f32[24,4096]{1,0:T(8,128)}, f32[24,4096]{1,0:T(8,128)}, u32[]{:S(2)}, u32[]{:S(2)}) collective-permute-start(f32[24,4096]{1,0:T(8,128)} %get-tuple-element.39), channel_id=1, source_target_pairs={{0,0},{1,1},{2,8},{3,9},{4,16},{5,17},{6,24},{7,25},{8,2},{9,3},{1... | collective-permute-start | bytes 1179656 | tf_op jit(solution)/shard_map/ppermute | solution.py:113
  134.6 8.5 %collective-permute-start.11 = (f32[24,4096]{1,0:T(8,128)S(1)}, f32[24,4096]{1,0:T(8,128)}, u32[]{:S(2)}, u32[]{:S(2)}) collective-permute-start(f32[24,4096]{1,0:T(8,128)S(1)} %get-tuple-element.38), channel_id=1, source_target_pairs={{0,1},{1,0},{2,9},{3,8},{4,17},{5,16},{6,25},{7,24},{8,3},{9,2},{1... | collective-permute-start | bytes 1179656 | tf_op jit(solution)/shard_map/ppermute | solution.py:113
  144.9 35.2 %collective-permute-start.12 = (bf16[48,4096]{1,0:T(8,128)(2,1)S(1)}, bf16[48,4096]{1,0:T(8,128)(2,1)S(1)}, u32[]{:S(2)}, u32[]{:S(2)}) collective-permute-start(bf16[48,4096]{1,0:T(8,128)(2,1)S(1)} %fusion.24), channel_id=1, source_target_pairs={{0,16},{8,24},{16,0},{24,8},{1,17},{9,25},{17,1},{25,9},{2,18},{10... | collective-permute-start | bytes 1179656 | tf_op jit(solution)/shard_map/ppermute | solution.py:32
  181.5 12.4 %collective-permute-start.13 = (bf16[2,48,4096]{2,1,0:T(8,128)(2,1)}, bf16[2,48,4096]{2,1,0:T(8,128)(2,1)}, u32[]{:S(2)}, u32[]{:S(2)}) collective-permute-start(bf16[2,48,4096]{2,1,0:T(8,128)(2,1)} %fusion.36), channel_id=1, source_target_pairs={{0,8},{8,0},{16,24},{24,16},{1,9},{9,1},{17,25},{25,17},{2,10},{10... | collective-permute-start | bytes 2359304 | tf_op jit(solution)/shard_map/ppermute | solution.py:34
  181.6 3.6 %collective-permute-start.14 = (f32[1,2,24]{2,1,0:T(2,128)S(1)}, f32[1,2,24]{2,1,0:T(2,128)S(1)}, u32[]{:S(2)}, u32[]{:S(2)}) collective-permute-start(f32[1,2,24]{2,1,0:T(2,128)S(1)} %bitcast.168), channel_id=1, source_target_pairs={{0,1},{1,0},{2,3},{3,2},{4,5},{5,4},{6,7},{7,6},{8,9},{9,8},{10,11... | collective-permute-start | bytes 584 | tf_op jit(solution)/shard_map/ppermute | solution.py:22
  185.2 3.6 %collective-permute-start.15 = (f32[2,2,24]{2,1,0:T(2,128)S(1)}, f32[2,2,24]{2,1,0:T(2,128)S(1)}, u32[]{:S(2)}, u32[]{:S(2)}) collective-permute-start(f32[2,2,24]{2,1,0:T(2,128)S(1)} %maximum_select_fusion.3), channel_id=1, source_target_pairs={{0,2},{1,3},{2,0},{3,1},{4,6},{5,7},{6,4},{7,5},{8,10},{9,11},{10,... | collective-permute-start | bytes 1160 | tf_op jit(solution)/shard_map/ppermute | solution.py:22
  188.8 4.9 %collective-permute-start.16 = (f32[4,2,24]{2,1,0:T(2,128)S(1)}, f32[4,2,24]{2,1,0:T(2,128)S(1)}, u32[]{:S(2)}, u32[]{:S(2)}) collective-permute-start(f32[4,2,24]{2,1,0:T(2,128)S(1)} %maximum_select_fusion.1), channel_id=1, source_target_pairs={{0,4},{1,5},{2,6},{3,7},{4,0},{5,1},{6,2},{7,3},{8,12},{9,13},{10,... | collective-permute-start | bytes 2312 | tf_op jit(solution)/shard_map/ppermute | solution.py:22
  233.3 38.9 %copy-start.4 = (f32[192,4096]{1,0:T(8,128)S(1)}, f32[192,4096]{1,0:T(8,128)}, u32[]{:S(2)}) copy-start(f32[192,4096]{1,0:T(8,128)} %fusion.21) | copy-start | bytes 9437188
  234.9 37.3 %collective-permute-start.21 = (f16[4,24,4096]{2,1,0:T(8,128)(2,1)S(1)}, f16[4,24,4096]{2,1,0:T(8,128)(2,1)S(1)}, u32[]{:S(2)}, u32[]{:S(2)}) collective-permute-start(f16[4,24,4096]{2,1,0:T(8,128)(2,1)S(1)} %fusion.33), channel_id=1, source_target_pairs={{0,1},{1,0},{2,3},{3,2},{4,5},{5,4},{6,7},{7,6},{8,9},{9,8},{10,11... | collective-permute-start | bytes 2359304 | tf_op jit(solution)/shard_map/ppermute | solution.py:49
  236.0 56.7 %collective-permute-start.17 = (f16[4,24,4096]{2,1,0:T(8,128)(2,1)S(1)}, f16[4,24,4096]{2,1,0:T(8,128)(2,1)S(1)}, u32[]{:S(2)}, u32[]{:S(2)}) collective-permute-start(f16[4,24,4096]{2,1,0:T(8,128)(2,1)S(1)} %copy-done.8), channel_id=1, source_target_pairs={{0,1},{1,0},{2,3},{3,2},{4,5},{5,4},{6,7},{7,6},{8,9},{9,8},{10,11... | collective-permute-start | bytes 2359304 | tf_op jit(solution)/shard_map/ppermute | solution.py:49
  272.6 23.9 %collective-permute-start.24 = (f16[24,4096]{1,0:T(8,128)(2,1)S(1)}, f16[24,4096]{1,0:T(8,128)(2,1)S(1)}, u32[]{:S(2)}, u32[]{:S(2)}) collective-permute-start(f16[24,4096]{1,0:T(8,128)(2,1)S(1)} %get-tuple-element.36), channel_id=1, source_target_pairs={{0,6},{1,7},{2,0},{3,1},{4,2},{5,3},{6,4},{7,5},{8,14},{9,15},{10,... | collective-permute-start | bytes 589832 | tf_op jit(solution)/shard_map/ppermute | solution.py:56
  275.4 30.4 %collective-permute-start.23 = (f16[24,4096]{1,0:T(8,128)(2,1)S(1)}, f16[24,4096]{1,0:T(8,128)(2,1)S(1)}, u32[]{:S(2)}, u32[]{:S(2)}) collective-permute-start(f16[24,4096]{1,0:T(8,128)(2,1)S(1)} %get-tuple-element.37), channel_id=1, source_target_pairs={{0,4},{1,5},{2,6},{3,7},{4,0},{5,1},{6,2},{7,3},{8,12},{9,13},{10,... | collective-permute-start | bytes 589832 | tf_op jit(solution)/shard_map/ppermute | solution.py:56
  275.7 30.0 %collective-permute-start.22 = (f16[24,4096]{1,0:T(8,128)(2,1)S(1)}, f16[24,4096]{1,0:T(8,128)(2,1)S(1)}, u32[]{:S(2)}, u32[]{:S(2)}) collective-permute-start(f16[24,4096]{1,0:T(8,128)(2,1)S(1)} %get-tuple-element.35), channel_id=1, source_target_pairs={{0,2},{1,3},{2,4},{3,5},{4,6},{5,7},{6,0},{7,1},{8,10},{9,11},{10,... | collective-permute-start | bytes 589832 | tf_op jit(solution)/shard_map/ppermute | solution.py:56
  293.1 31.0 %copy-start.6 = (bf16[2,24,8192]{2,1,0:T(8,128)(2,1)S(1)}, bf16[2,24,8192]{2,1,0:T(8,128)(2,1)}, u32[]{:S(2)}) copy-start(bf16[2,24,8192]{2,1,0:T(8,128)(2,1)} %param.8) | copy-start | bytes 2359300
  293.1 14.7 %collective-permute-start.20 = (f16[24,4096]{1,0:T(8,128)(2,1)S(1)}, f16[24,4096]{1,0:T(8,128)(2,1)S(1)}, u32[]{:S(2)}, u32[]{:S(2)}) collective-permute-start(f16[24,4096]{1,0:T(8,128)(2,1)S(1)} %get-tuple-element.33), channel_id=1, source_target_pairs={{0,6},{1,7},{2,0},{3,1},{4,2},{5,3},{6,4},{7,5},{8,14},{9,15},{10,... | collective-permute-start | bytes 589832 | tf_op jit(solution)/shard_map/ppermute | solution.py:56
  296.4 27.5 %collective-permute-start.19 = (f16[24,4096]{1,0:T(8,128)(2,1)S(1)}, f16[24,4096]{1,0:T(8,128)(2,1)S(1)}, u32[]{:S(2)}, u32[]{:S(2)}) collective-permute-start(f16[24,4096]{1,0:T(8,128)(2,1)S(1)} %get-tuple-element.34), channel_id=1, source_target_pairs={{0,4},{1,5},{2,6},{3,7},{4,0},{5,1},{6,2},{7,3},{8,12},{9,13},{10,... | collective-permute-start | bytes 589832 | tf_op jit(solution)/shard_map/ppermute | solution.py:56
  296.5 27.5 %collective-permute-start.18 = (f16[24,4096]{1,0:T(8,128)(2,1)S(1)}, f16[24,4096]{1,0:T(8,128)(2,1)S(1)}, u32[]{:S(2)}, u32[]{:S(2)}) collective-permute-start(f16[24,4096]{1,0:T(8,128)(2,1)S(1)} %get-tuple-element.32), channel_id=1, source_target_pairs={{0,2},{1,3},{2,4},{3,5},{4,6},{5,7},{6,0},{7,1},{8,10},{9,11},{10,... | collective-permute-start | bytes 589832 | tf_op jit(solution)/shard_map/ppermute | solution.py:56
  330.6 3.6 %collective-permute-start.25 = (f32[1,2,24]{2,1,0:T(2,128)S(1)}, f32[1,2,24]{2,1,0:T(2,128)S(1)}, u32[]{:S(2)}, u32[]{:S(2)}) collective-permute-start(f32[1,2,24]{2,1,0:T(2,128)S(1)} %bitcast.170), channel_id=1, source_target_pairs={{0,1},{1,0},{2,3},{3,2},{4,5},{5,4},{6,7},{7,6},{8,9},{9,8},{10,11... | collective-permute-start | bytes 584 | tf_op jit(solution)/shard_map/ppermute | solution.py:22
  334.3 3.6 %collective-permute-start.26 = (f32[2,2,24]{2,1,0:T(2,128)S(1)}, f32[2,2,24]{2,1,0:T(2,128)S(1)}, u32[]{:S(2)}, u32[]{:S(2)}) collective-permute-start(f32[2,2,24]{2,1,0:T(2,128)S(1)} %maximum_select_fusion.4), channel_id=1, source_target_pairs={{0,2},{1,3},{2,0},{3,1},{4,6},{5,7},{6,4},{7,5},{8,10},{9,11},{10,... | collective-permute-start | bytes 1160 | tf_op jit(solution)/shard_map/ppermute | solution.py:22
  337.8 4.5 %collective-permute-start.27 = (f32[4,2,24]{2,1,0:T(2,128)S(1)}, f32[4,2,24]{2,1,0:T(2,128)S(1)}, u32[]{:S(2)}, u32[]{:S(2)}) collective-permute-start(f32[4,2,24]{2,1,0:T(2,128)S(1)} %maximum_select_fusion.2), channel_id=1, source_target_pairs={{0,4},{1,5},{2,6},{3,7},{4,0},{5,1},{6,2},{7,3},{8,12},{9,13},{10,... | collective-permute-start | bytes 2312 | tf_op jit(solution)/shard_map/ppermute | solution.py:22
  (7 other events, 61.6 us)
Sparse Core Ops, SparseCore 0:
  181.7 138.5 all-gather.1
